TPU v7x, 32 devices: a whole 2x2x4 slice. The times are simulated.
32 devices in a mesh: group: 2 (over y), tm: 4 (over x, core), space: 4 (over z).
Axes of the slice: x: 2, y: 2, z: 4, core: 2. Of those that a mesh axis runs over, the one named last changes fastest.
Arguments:
- start_latent: float32 [32, 32, 256], P('group', 'space'), parts along dimension 0, may hold values from -6 to 6
- time_embed: float32 [8, 128], P('tm'), may hold values from -6 to 6
- drift_x: float32 [8], P('tm'), may hold values from -0.06 to -0.01
- drift_eps: float32 [8], P('tm'), may hold values from 0.02 to 0.1
- w_in: float32 [3, 3, 128, 16], replicated, may hold values from -0.5 to 0.5
- b_in: float32 [128], replicated, may hold values from -3 to 3
- w_mid: float32 [3, 3, 128, 128], replicated, may hold values from -0.1875 to 0.1875
- b_mid: float32 [128], replicated, may hold values from -3 to 3
- w_out: float32 [3, 3, 16, 128], replicated, may hold values from -0.1875 to 0.1875
- b_out: float32 [16], replicated, may hold values from -3 to 3
Outputs:
- trajectory: float32 [8, 32, 32, 256], P('tm', 'group', 'space'), parts along dimension 1
There are 2 independent parts, one for each index of `group`. A program takes and returns all parts, laid end to end along the dimension named above; an argument that names none is the same for every part. Nothing has to cross between parts.
All inputs are finite; a program needn't handle non-finite values.
Results may differ from a plain program's by a relative error of at most 0.0001.
Values sent between devices are 32-bit elements; how exact they have to be, the bound alone decides.
No kernel may reach another device: no remote copies, remote signals or barrier semaphores. Data moves between devices by JAX's collectives and lax.ppermute only.
A program may use at most 64 MiB of HBM per device.

v0:
```python
import functools
import jax
import jax.numpy as jnp
from jax import lax
from jax.experimental import pallas as pl
from jax.experimental.pallas import tpu as pltpu
from jax.sharding import PartitionSpec as P

REACH = 3
HALO = 2 * REACH
OFF = -1e30
VMEM_LIMIT = 56 * 2**20
F32, BF16 = jnp.float32, jnp.bfloat16


def split(value):
    high = value.astype(BF16)
    return high, (value - high.astype(F32)).astype(BF16)


def silu(value):
    half = 0.5 * value
    return half + half * jnp.tanh(half)


def lane_groups(shape, size):
    return lax.broadcasted_iota(jnp.int32, shape, len(shape) - 1) // size


def weights_kernel(wi_ref, wm_ref, wo_ref, wi_out, wm_out, wo_out):
    depth = wi_ref.shape[0]
    high, low = split(wi_ref[...])
    rest = jnp.zeros((wi_out.shape[0] - 3 * depth, wi_ref.shape[1]), BF16)
    wi_out[...] = jnp.concatenate([high, high, low, rest], 0)
    hid = wm_ref.shape[-1]
    for a in range(3):
        w0, w1, w2 = (wm_ref[a, b].T for b in range(3))
        even, odd = w0 * (1 / 24) + w2 * (1 / 6), w1 * (1 / 12)
        sides = (w0 + w2) * (-1 / 6)
        middle = w1 * (-1 / 6)
        forms = (w0 * 0.25, sides + middle, sides - middle, even + odd, even - odd, w2)
        for point, form in enumerate(forms):
            both = jnp.concatenate(split(form), 1)
            wm_out[point, 2 * a * hid : (2 * a + 1) * hid] = both
            wm_out[point, (2 * a + 1) * hid : (2 * a + 2) * hid] = both
        out = wo_ref[a]
        high = out.astype(BF16).astype(F32)
        third = lane_groups(out.shape, out.shape[-1] // 8) < 3
        both = jnp.where(third, high, out - high).astype(BF16)
        wo_out[2 * a * hid : (2 * a + 1) * hid] = both
        wo_out[(2 * a + 1) * hid : (2 * a + 2) * hid] = both


def main_kernel(
    tm, up_ref, mid_ref, down_ref, par_ref, bias_ref, wi_ref, wm_ref, wo_ref, *refs
):
    outs = refs[:tm]
    start_s, points_s, hid2_s, inputs_s, packed_s, chunk_s, in_bias, mid_bias, eps_s = refs[tm:]
    rows, chans = mid_ref.shape[0], mid_ref.shape[1]
    states, hid = par_ref.shape[0], wm_ref.shape[2] // 2
    groups = points_s.shape[2] // states
    wide = 4 * groups
    cols = wide - 8
    my_tm, my_space = lax.axis_index("tm"), lax.axis_index("space")
    all_rows, all_cols = rows * lax.axis_size("space"), cols * tm
    row0, col0 = my_space * rows, my_tm * cols
    replicas = hid // chans

    embed, drift_x, drift_eps = par_ref[:, :hid], par_ref[:, hid : hid + 1], par_ref[:, hid + 1 : hid + 2]
    drift_x = jnp.broadcast_to(drift_x, (states, hid))

    def inside(first, width, limit):
        place = lax.broadcasted_iota(jnp.int32, (width, states, hid), 0)
        return (place + first >= 0) & (place + first < all_cols) & (place < limit)

    bias = bias_ref[0:1] + embed
    in_bias[0] = jnp.full(in_bias.shape[1:], OFF, F32)
    in_bias[1] = jnp.where(inside(col0 - 5, wide + 4, wide + 2), bias[None], OFF)
    mid_bias[0] = jnp.full(mid_bias.shape[1:], OFF, F32)
    mid_bias[1] = jnp.where(
        inside(col0 - 4, mid_bias.shape[1], mid_bias.shape[1]),
        jnp.broadcast_to(bias_ref[1:2], (states, hid))[None],
        OFF,
    )
    eps_s[0] = jnp.zeros(eps_s.shape[1:], F32)
    eps_s[1] = jnp.where(
        inside(col0 - 3, wide, wide), jnp.broadcast_to(drift_eps, (states, hid))[None], 0.0
    )
    out_bias = bias_ref[2:3]

    def in_field(row):
        return jnp.where((row >= 0) & (row < all_rows), 1, 0)

    for ref, first in ((up_ref, 0), (mid_ref, HALO), (down_ref, HALO + rows)):

        def turn(i, _, ref=ref, first=first):
            start_s[first + i] = jnp.concatenate([ref[i]] * replicas, 0).T
            return 0

        lax.fori_loop(0, ref.shape[0], turn, 0)

    def stacked(r0, r1, r2):
        place = lane_groups(r0.shape, chans)
        value = jnp.where(place % 3 == 0, r0, jnp.where(place % 3 == 1, r1, r2))
        high = value.astype(BF16).astype(F32)
        low_part = (place >= 3) & (place < 6)
        return jnp.concatenate(
            [jnp.where(low_part, value - high, value).astype(BF16), r2.astype(BF16)], 1
        )

    def first_conv(left):
        return jnp.dot(left, wi_ref[...], preferred_element_type=F32)

    def to_points(row, field):
        fours = field.reshape(groups + 1, 4, states, hid)
        d0, d1, d2, d3 = (fours[:groups, k] for k in range(4))
        d4, d5 = fours[1:, 0], fours[1:, 1]
        e1, e2 = d4 - 4 * d2, d3 - 4 * d1
        e3, e4 = d4 - d2, 2 * (d3 - d1)
        forms = (4 * d0 - 5 * d2 + d4, e1 + e2, e1 - e2, e3 + e4, e3 - e4, 4 * d1 - 5 * d3 + d5)
        for point, form in enumerate(forms):
            high, low = split(form.reshape(groups * states, hid))
            points_s[point, row, :, :hid] = high
            points_s[point, row, :, hid:] = low

    def second_hidden(count, step, row_first, col_first):
        def body(c, _):
            first = c * step
            sums = []
            for point in range(6):
                left = jnp.concatenate(
                    [
                        points_s[point, pl.ds(first + a, step)].reshape(step * groups * states, 2 * hid)
                        for a in range(3)
                    ],
                    1,
                )
                both = jnp.dot(left, wm_ref[point], preferred_element_type=F32)
                sums.append((both[:, :hid] + both[:, hid:]).reshape(step, groups, states, hid))
            m0, m1, m2, m3, m4, m5 = sums
            s1, t1, s3, t3 = m1 + m2, m1 - m2, m3 + m4, m3 - m4
            field = jnp.stack(
                [m0 + s1 + s3, t1 + 2 * t3, s1 + 4 * s3, t1 + 8 * t3 + m5], 2
            ).reshape(step, wide, states, hid)
            for r in range(step):
                ok = in_field(row0 + row_first + first + r)
                value = silu(field[r] + mid_bias[ok, col_first : col_first + wide])
                high, low = split(value.reshape(wide * states, hid))
                hid2_s[first + r, :, :hid] = high
                hid2_s[first + r, :, hid:] = low
            return 0

        lax.fori_loop(0, count // step, body, 0)

    def noise(first, step, width):
        left = jnp.concatenate(
            [
                hid2_s[pl.ds(first + a, step)].reshape(step * wide * states, 2 * hid)
                for a in range(3)
            ],
            1,
        )
        taps = jnp.dot(left, wo_ref[...], preferred_element_type=F32)
        taps = taps.reshape(step, wide, states, hid)
        shape = (step, width, states, hid)
        place = lane_groups(shape, chans) % 3
        value = jnp.where(
            place == 0,
            taps[:, 0:width],
            jnp.where(place == 1, taps[:, 1 : width + 1], taps[:, 2 : width + 2]),
        ).reshape(step * width * states, hid)
        size = hid // 2
        while size >= chans:
            value = value + pltpu.roll(value, size, 1)
            size //= 2
        return (value + out_bias).reshape(shape)

    state = lax.broadcasted_iota(jnp.int32, (1, states, hid), 1)

    def earlier(value):
        value = jnp.where(state >= 1, pltpu.roll(value, 1, 1), 0.0)
        reach = 1
        while reach < states:
            value = value + jnp.where(state >= reach, pltpu.roll(value, reach, 1), 0.0)
            reach *= 2
        return value

    def first_rows(i, _):
        depth = start_s.shape[1]
        left = stacked(start_s[i], start_s[i + 1], start_s[i + 2])
        taps = first_conv(left)
        t0, t1, t2 = (taps[:, k * hid : (k + 1) * hid] for k in range(3))
        common = t0 + pltpu.roll(t1, depth - 1, 0) + pltpu.roll(t2, depth - 2, 0)
        ok = in_field(row0 - 5 + i)
        to_points(i, silu(common[: wide + 4, None, :] + in_bias[ok]))
        return 0

    lax.fori_loop(0, rows + 10, first_rows, 0)
    second_hidden(rows + 8, 4 if rows % 4 == 0 else 1, -4, 0)
    reach_cols = cols + HALO

    def next_inputs(i, _):
        value = noise(i, 1, reach_cols)[0]
        ok = in_field(row0 - REACH + i)
        start = jnp.broadcast_to(
            start_s[REACH + i, REACH : REACH + reach_cols, :][:, None, :], (reach_cols, states, hid)
        )
        drift = drift_x[None] * start + eps_s[ok, :reach_cols] * value
        value = (start + earlier(drift)).reshape(reach_cols * states, hid)
        inputs_s[i, : reach_cols * states] = value
        inputs_s[i, reach_cols * states :] = jnp.zeros(((wide - reach_cols) * states, hid), F32)
        return 0

    lax.fori_loop(0, rows + HALO, next_inputs, 0)

    def second_rows(i, _):
        taps = first_conv(stacked(inputs_s[i], inputs_s[i + 1], inputs_s[i + 2]))
        width = cols + 4
        t0, t1, t2 = (
            taps[k * states : (k + width) * states, k * hid : (k + 1) * hid] for k in range(3)
        )
        ok = in_field(row0 - 2 + i)
        value = silu((t0 + t1 + t2).reshape(width, states, hid) + in_bias[ok, 3 : 3 + width])
        to_points(i, jnp.concatenate([value, jnp.zeros((8, states, hid), F32)], 0))
        return 0

    lax.fori_loop(0, rows + 4, second_rows, 0)
    second_hidden(rows + 2, 5 if (rows + 2) % 5 == 0 else 1, -1, 3)

    packed = jnp.zeros((cols * states, hid), F32)
    place = lane_groups((cols * states, hid), chans)
    packed_s[...] = packed

    def last_rows(i, _):
        value = noise(i, 1, cols)[0]
        here = inputs_s[REACH + i, REACH * states : (REACH + cols) * states]
        drift = drift_x[None] * here.reshape(cols, states, hid) + drift_eps[None] * value
        packed_s[...] = jnp.where(place == i, drift.reshape(cols * states, hid), packed_s[...])
        return 0

    lax.fori_loop(0, rows, last_rows, 0)

    size = cols * states
    source = lax.broadcasted_iota(jnp.int32, (size, size), 0)
    target = lax.broadcasted_iota(jnp.int32, (size, size), 1)
    same = (source // states) == (target % cols)
    upto = (source % states) <= (target // cols)
    sums = jnp.where(same & upto, 1.0, 0.0).astype(BF16)
    high, low = split(packed_s[...].T)
    total = jnp.dot(high, sums, preferred_element_type=F32) + jnp.dot(
        low, sums, preferred_element_type=F32
    )
    start = mid_ref[...].reshape(rows * chans, mid_ref.shape[2])[:, HALO : HALO + cols]
    here = states // tm
    start = jnp.concatenate([start] * here, 1)
    width = here * cols
    for k in range(tm):
        value = start + total[:, k * width : (k + 1) * width]
        for r in range(rows):
            chunk_s[k, :, r, :] = value[r * chans : (r + 1) * chans]
    for k in range(tm):
        outs[k][...] = chunk_s[my_tm ^ k]


def join_kernel(tm, *refs):
    blocks, out_ref, held = refs[:tm], refs[tm], refs[tm + 1]
    here = out_ref.shape[0]
    cols = out_ref.shape[3] // tm
    for k in range(tm):
        held[k] = blocks[k][...]
    my_tm = lax.axis_index("tm")
    for k in range(tm):
        block = held[my_tm ^ k]
        for t in range(here):
            out_ref[t, :, :, k * cols : (k + 1) * cols] = block[:, :, t * cols : (t + 1) * cols]


def kernel_call(body, out_shape, count, scratch=(), flops=0, read=0):
    vmem = pl.BlockSpec(memory_space=pltpu.VMEM)
    return pl.pallas_call(
        body,
        out_shape=out_shape,
        in_specs=[vmem] * count,
        out_specs=jax.tree.map(lambda _: vmem, out_shape),
        scratch_shapes=list(scratch),
        compiler_params=pltpu.CompilerParams(vmem_limit_bytes=VMEM_LIMIT),
        cost_estimate=pl.CostEstimate(flops=flops, bytes_accessed=read, transcendentals=0),
    )


def on_device(start_latent, time_embed, drift_x, drift_eps, w_in, b_in, w_mid, b_mid, w_out, b_out):
    tm, space = lax.axis_size("tm"), lax.axis_size("space")
    my_tm = lax.axis_index("tm")
    chans, rows, all_cols = start_latent.shape
    here, hid = time_embed.shape
    states, cols = here * tm, all_cols // tm
    depth = -(-(cols + 2 * HALO) // 128) * 128
    shape = jax.ShapeDtypeStruct

    padded = jnp.pad(start_latent, ((0, 0), (0, 0), (HALO, depth - cols - HALO)))
    mid = lax.dynamic_slice_in_dim(padded, my_tm * cols, depth, 2).transpose(1, 0, 2)
    up = lax.ppermute(mid[rows - HALO :], "space", [(i, i + 1) for i in range(space - 1)])
    down = lax.ppermute(mid[:HALO], "space", [(i + 1, i) for i in range(space - 1)])
    par = jnp.concatenate(
        [time_embed, drift_x[:, None], drift_eps[:, None], jnp.zeros((here, hid - 2), F32)], 1
    )
    par = lax.all_gather(par, "tm", tiled=True)

    wi = w_in.transpose(0, 3, 1, 2).reshape(3 * chans, 3 * hid)
    wo = w_out.transpose(0, 3, 1, 2).reshape(3, hid, 3 * chans)
    wo = jnp.concatenate([wo, wo, jnp.zeros((3, hid, hid - 6 * chans), F32)], 2)
    wi, wm, wo = kernel_call(
        weights_kernel,
        (
            shape((2 * hid, 3 * hid), BF16),
            shape((6, 6 * hid, 2 * hid), BF16),
            shape((6 * hid, hid), BF16),
        ),
        3,
        flops=10**7,
        read=3 * 10**6,
    )(wi, w_mid, wo)
    bias = jnp.stack([b_in, b_mid, jnp.tile(b_out, hid // chans)] + [b_in] * 5)

    groups = (cols + 8) // 4
    wide = 4 * groups
    width = here * cols
    chunks = kernel_call(
        functools.partial(main_kernel, tm),
        tuple(shape((chans, rows, width), F32) for _ in range(tm)),
        8,
        scratch=(
            pltpu.VMEM((rows + 2 * HALO, depth, hid), F32),
            pltpu.VMEM((6, rows + 10, groups * states, 2 * hid), BF16),
            pltpu.VMEM((rows + 8, wide * states, 2 * hid), BF16),
            pltpu.VMEM((rows + HALO, wide * states, hid), F32),
            pltpu.VMEM((cols * states, hid), F32),
            pltpu.VMEM((tm, chans, rows, width), F32),
            pltpu.VMEM((2, wide + 4, states, hid), F32),
            pltpu.VMEM((2, wide + 3, states, hid), F32),
            pltpu.VMEM((2, wide, states, hid), F32),
        ),
        flops=10**10,
        read=4 * 10**6,
    )(up, mid, down, par, bias, wi, wm, wo)

    blocks = [chunks[0]] + [
        lax.ppermute(chunks[k], "tm", [(i, i ^ k) for i in range(tm)]) for k in range(1, tm)
    ]
    return kernel_call(
        functools.partial(join_kernel, tm),
        shape((here, chans, rows, all_cols), F32),
        tm,
        scratch=(pltpu.VMEM((tm, chans, rows, width), F32),),
        read=10**6,
    )(*blocks)


def solution(mesh):
    in_specs = (
        P("group", "space", None),
        P("tm", None),
        P("tm"),
        P("tm"),
        P(),
        P(),
        P(),
        P(),
        P(),
        P(),
    )
    out_specs = P("tm", "group", "space", None)
    return jax.shard_map(
        on_device, mesh=mesh, in_specs=in_specs, out_specs=out_specs, check_vma=False
    )
```

profile of v0, /device:TPU:9, one launch (start us, length us, event | category | flops | bytes accessed | tf_op | source)
XLA Modules:
  0.0 79.3 jit_solution(11902027185068753914)
XLA Ops:
  0.0 0.9 %copy.22 = f32[16,8,256]{2,0,1:T(8,128)S(1)} copy(f32[16,8,256]{2,1,0:T(8,128)} %param.10) | data formatting | bytes 262144 | tf_op args[0]
  1.0 0.1 fusion.mid_ref
  1.0 0.0 copy-start
  1.1 3.2 %collective-permute-start = (f32[6,16,128]{2,1,0:T(8,128)S(1)}, f32[6,16,128]{2,1,0:T(8,128)S(1)}, u32[]{:S(2)}, u32[]{:S(2)}) collective-permute-start(f32[6,16,128]{2,1,0:T(8,128)S(1)} %get-tuple-element.20), channel_id=1, source_target_pairs={{0,1},{1,2},{2,3},{4,5},{5,6},{6,7},{8,9},{9,10},{10,11},{12,13},{... | collective-permute-start | bytes 147464 | tf_op jit(solution)/shard_map/ppermute | solution.py:302
  4.3 2.1 %collective-permute-start.1 = (f32[6,16,128]{2,1,0:T(8,128)S(1)}, f32[6,16,128]{2,1,0:T(8,128)S(1)}, u32[]{:S(2)}, u32[]{:S(2)}) collective-permute-start(f32[6,16,128]{2,1,0:T(8,128)S(1)} %get-tuple-element.19), channel_id=1, source_target_pairs={{1,0},{2,1},{3,2},{5,4},{6,5},{7,6},{9,8},{10,9},{11,10},{13,12},{... | collective-permute-start | bytes 147464 | tf_op jit(solution)/shard_map/ppermute | solution.py:303
  6.4 1.0 %copy.26 = f32[3,128,48]{2,1,0:T(8,128)S(1)} copy(f32[3,128,48]{1,2,0:T(8,128)} %bitcast.19) | data formatting | bytes 147456 | tf_op jit(solution)/shard_map/reshape | solution.py:310
  7.4 0.1 pad.7.clone
  7.5 0.1 pad.11.clone
  7.5 0.7 copy.23
  8.3 0.7 copy.24
  9.0 0.8 %maximum_maximum_fusion.wo_ref = f32[3,128,128]{2,1,0:T(8,128)} fusion(f32[3,128,48]{2,1,0:T(8,128)S(1)} %copy.26, f32[128]{0:T(128)S(1)} %pad.7.clone), kind=kLoop, calls=%fused_computation | loop fusion | flops 98304 | bytes 270848 | tf_op jit(solution)/shard_map/concatenate | solution.py:311
  9.8 0.8 maximum_bitcast_fusion
  10.6 0.9 %copy.25 = f32[3,16,3,128]{3,2,1,0:T(4,128)S(1)} copy(f32[3,16,3,128]{3,1,2,0:T(8,128)} %bitcast.20) | data formatting | bytes 147456 | tf_op jit(solution)/shard_map/transpose | solution.py:309
  11.5 0.6 copy.30
  12.1 6.2 %all-gather = f32[4,2,256]{2,1,0:T(2,128)S(1)} all-gather(f32[1,2,256]{2,1,0:T(2,128)S(1)} %maximum_bitcast_fusion), channel_id=1, replica_groups=mesh['group'=2,'tm'=4,'space'=4] {'tm'}, dimensions={0}, use_global_device_ids=true | all-gather | bytes 10240 | tf_op jit(solution)/shard_map/all_gather | solution.py:307
  18.3 0.6 reshape.10.par_ref
  18.9 0.7 tile.2
  19.6 0.1 stack_tile.3
  19.7 1.5 %stack.16.bias_ref = f32[8,128]{1,0:T(8,128)} concatenate(f32[1,128]{1,0:T(1,128)} %bitcast.21, f32[1,128]{1,0:T(1,128)} %bitcast.27, f32[1,128]{1,0:T(1,128)S(1)} %stack_tile.3, f32[1,128]{1,0:T(1,128)} %bitcast.22, f32[1,128]{1,0:T(1,128)} %bitcast.23, f32[1,128]{1,0:T(1,128)} %bitcast.24, f32[1,128]{1,0:T(1,128)} %bitcast.25, f32[1,128]{1,0:T(1,128)} %bitcast.26), dimensions={0} | concatenate | bytes 8192 | tf_op jit(solution)/shard_map/stack | solution.py:323
  21.1 3.0 %shard_map.100 = (bf16[256,384]{1,0:T(8,128)(2,1)}, bf16[6,768,256]{2,1,0:T(8,128)(2,1)}, bf16[768,128]{1,0:T(8,128)(2,1)}) custom-call(f32[48,384]{1,0:T(8,128)} %bitcast.18, f32[3,3,128,128]{3,2,1,0:T(8,128)} %wm_ref.1, f32[3,128,128]{2,1,0:T(8,128)} %maximum_maximum_fusion.wo_ref), custom_call_target="tpu_custom_call" | custom-call | flops 10000000 | bytes 3000000 | tf_op jit(solution)/shard_map/pallas_call | solution.py:312
  24.1 0.0 collective-permute-done.up_ref
  24.1 0.0 copy-start.4
  24.1 0.0 collective-permute-done.1.down_ref
  24.1 0.0 copy-start.5
  24.1 0.0 copy-done
  24.1 0.6 copy-done.4
  24.7 0.0 copy-done.5
  24.7 46.0 %shard_map.101 = (f32[16,8,128]{2,1,0:T(8,128)}, f32[16,8,128]{2,1,0:T(8,128)}, f32[16,8,128]{2,1,0:T(8,128)}, f32[16,8,128]{2,1,0:T(8,128)}) custom-call(f32[6,16,128]{2,1,0:T(8,128)} %copy-done.4, f32[8,16,128]{2,1,0:T(8,128)} %copy-done, f32[6,16,128]{2,1,0:T(8,128)} %copy-done.5, f32[8,256]{1,0:T(8,128)} %reshape.10.par_ref, f32[8,128]{1,0:T(8,128)} %stack.16.bias_ref, ...), custom_call_target="tpu_custom_call" | custom-call | flops 10000000000 | bytes 4000000 | tf_op jit(solution)/shard_map/pallas_call | solution.py:328
  70.7 0.2 collective-permute-start.2
  71.0 1.2 %collective-permute-start.3 = (f32[16,8,128]{2,1,0:T(8,128)}, f32[16,8,128]{2,1,0:T(8,128)S(1)}, u32[]{:S(2)}, u32[]{:S(2)}) collective-permute-start(f32[16,8,128]{2,1,0:T(8,128)} %get-tuple-element.17), channel_id=1, source_target_pairs={{0,8},{4,12},{8,0},{12,4},{1,9},{5,13},{9,1},{13,5},{2,10},{6,14},... | collective-permute-start | bytes 196616 | tf_op jit(solution)/shard_map/ppermute | solution.py:348
  72.2 0.7 collective-permute-start.4
  72.9 0.0 collective-permute-done.2.refs_1_
  72.9 0.0 copy-start.1
  72.9 1.4 %collective-permute-done.3.refs_2_ = f32[16,8,128]{2,1,0:T(8,128)S(1)} collective-permute-done((f32[16,8,128]{2,1,0:T(8,128)}, f32[16,8,128]{2,1,0:T(8,128)S(1)}, u32[]{:S(2)}, u32[]{:S(2)}) %collective-permute-start.3) | collective-permute-done | bytes 65568 | tf_op jit(solution)/shard_map/ppermute | solution.py:348
  74.3 0.0 copy-start.2
  74.3 2.6 %collective-permute-done.4.refs_3_ = f32[16,8,128]{2,1,0:T(8,128)S(1)} collective-permute-done((f32[16,8,128]{2,1,0:T(8,128)}, f32[16,8,128]{2,1,0:T(8,128)S(1)}, u32[]{:S(2)}, u32[]{:S(2)}) %collective-permute-start.4) | collective-permute-done | bytes 65568 | tf_op jit(solution)/shard_map/ppermute | solution.py:348
  76.9 0.0 copy-start.3
  76.9 0.0 copy-done.1
  76.9 0.0 copy-done.2
  76.9 0.6 copy-done.3
  77.5 1.8 %shard_map.102 = f32[2,16,8,256]{3,2,1,0:T(8,128)} custom-call(f32[16,8,128]{2,1,0:T(8,128)} %get-tuple-element.15.refs_0_, f32[16,8,128]{2,1,0:T(8,128)} %copy-done.1, f32[16,8,128]{2,1,0:T(8,128)} %copy-done.2, f32[16,8,128]{2,1,0:T(8,128)} %copy-done.3), custom_call_target="tpu_custom_call" | custom-call | bytes 1000000 | tf_op jit(solution)/shard_map/pallas_call | solution.py:350
  (3 shorter events, 0.0 us)
Async XLA Ops:
  1.0 23.1 %copy-start = (f32[8,16,128]{2,1,0:T(8,128)}, f32[8,16,128]{2,1,0:T(8,128)S(1)}, u32[]{:S(2)}) copy-start(f32[8,16,128]{2,1,0:T(8,128)S(1)} %fusion.mid_ref) | copy-start | bytes 196612
  1.1 23.1 %collective-permute-start = (f32[6,16,128]{2,1,0:T(8,128)S(1)}, f32[6,16,128]{2,1,0:T(8,128)S(1)}, u32[]{:S(2)}, u32[]{:S(2)}) collective-permute-start(f32[6,16,128]{2,1,0:T(8,128)S(1)} %get-tuple-element.20), channel_id=1, source_target_pairs={{0,1},{1,2},{2,3},{4,5},{5,6},{6,7},{8,9},{9,10},{10,11},{12,13},{... | collective-permute-start | bytes 147464 | tf_op jit(solution)/shard_map/ppermute | solution.py:302
  4.3 19.8 %collective-permute-start.1 = (f32[6,16,128]{2,1,0:T(8,128)S(1)}, f32[6,16,128]{2,1,0:T(8,128)S(1)}, u32[]{:S(2)}, u32[]{:S(2)}) collective-permute-start(f32[6,16,128]{2,1,0:T(8,128)S(1)} %get-tuple-element.19), channel_id=1, source_target_pairs={{1,0},{2,1},{3,2},{5,4},{6,5},{7,6},{9,8},{10,9},{11,10},{13,12},{... | collective-permute-start | bytes 147464 | tf_op jit(solution)/shard_map/ppermute | solution.py:303
  24.1 0.6 copy-start.4
  24.1 0.6 copy-start.5
  70.7 2.1 %collective-permute-start.2 = (f32[16,8,128]{2,1,0:T(8,128)}, f32[16,8,128]{2,1,0:T(8,128)S(1)}, u32[]{:S(2)}, u32[]{:S(2)}) collective-permute-start(f32[16,8,128]{2,1,0:T(8,128)} %get-tuple-element.16), channel_id=1, source_target_pairs={{0,4},{4,0},{8,12},{12,8},{1,5},{5,1},{9,13},{13,9},{2,6},{6,2},{1... | collective-permute-start | bytes 196616 | tf_op jit(solution)/shard_map/ppermute | solution.py:348
  71.0 3.3 %collective-permute-start.3 = (f32[16,8,128]{2,1,0:T(8,128)}, f32[16,8,128]{2,1,0:T(8,128)S(1)}, u32[]{:S(2)}, u32[]{:S(2)}) collective-permute-start(f32[16,8,128]{2,1,0:T(8,128)} %get-tuple-element.17), channel_id=1, source_target_pairs={{0,8},{4,12},{8,0},{12,4},{1,9},{5,13},{9,1},{13,5},{2,10},{6,14},... | collective-permute-start | bytes 196616 | tf_op jit(solution)/shard_map/ppermute | solution.py:348
  72.2 4.7 %collective-permute-start.4 = (f32[16,8,128]{2,1,0:T(8,128)}, f32[16,8,128]{2,1,0:T(8,128)S(1)}, u32[]{:S(2)}, u32[]{:S(2)}) collective-permute-start(f32[16,8,128]{2,1,0:T(8,128)} %get-tuple-element.18), channel_id=1, source_target_pairs={{0,12},{4,8},{8,4},{12,0},{1,13},{5,9},{9,5},{13,1},{2,14},{6,10},... | collective-permute-start | bytes 196616 | tf_op jit(solution)/shard_map/ppermute | solution.py:348
  72.9 4.0 %copy-start.1 = (f32[16,8,128]{2,1,0:T(8,128)}, f32[16,8,128]{2,1,0:T(8,128)S(1)}, u32[]{:S(2)}) copy-start(f32[16,8,128]{2,1,0:T(8,128)S(1)} %collective-permute-done.2.refs_1_) | copy-start | bytes 196612
  74.3 2.6 %copy-start.2 = (f32[16,8,128]{2,1,0:T(8,128)}, f32[16,8,128]{2,1,0:T(8,128)S(1)}, u32[]{:S(2)}) copy-start(f32[16,8,128]{2,1,0:T(8,128)S(1)} %collective-permute-done.3.refs_2_) | copy-start | bytes 196612
  76.9 0.6 copy-start.3
where the time goes:
time: 79.8 us; the launch traced here: 79.3 us
  Pallas kernels  50.8 us (64%)
  local copies, waits for them, and re-layouts  9.29 us (12%)
  starting transfers between devices  7.42 us (9%)
  blocking collectives  6.18 us (8%)
  waiting for transfers between devices  3.97 us (5%)
  other arithmetic  1.55 us (2%)
    pallas_call x1, Pallas kernels, on_device(): kernel_call(functools.partial(main_kernel, tm), tuple((shape((chans, rows...  46 us
    all_gather x1, blocking collectives, on_device(): par = lax.all_gather(par, 'tm', tiled=True)  6.18 us
    ppermute x3, waiting for transfers between devices, on_device(): lax.ppermute(chunks[k], 'tm', [(i, i ^ k) for i in range(tm)])  3.97 us
    unnamed x15, local copies, waits for them, and re-layouts  3.41 us
    ppermute x1, starting transfers between devices, on_device(): lax.ppermute(mid[rows - HALO:], 'space', [(i, i + 1) for i in range(space...  3.2 us
    pallas_call x1, Pallas kernels, on_device(): kernel_call(weights_kernel, (shape((2 * hid, 3 * hid), BF16), shape((6, 6...  2.99 us
    another operation x3, local copies, waits for them, and re-layouts, on_device(): bias = jnp.stack([b_in, b_mid, jnp.tile(b_out, hid // chans)] + [b_in] * 5)  2.21 us
    ppermute x3, starting transfers between devices, on_device(): lax.ppermute(chunks[k], 'tm', [(i, i ^ k) for i in range(tm)])  2.14 us
  transfers between devices with their start and end apart: 5, of which 2 were waited for; matrix products, arithmetic and copies ran while one was open for 11% of the time, Pallas kernels for 4%

commit v1 on v0

v1 whole, which is shorter than its diff:
```python
import functools
import jax
import jax.numpy as jnp
from jax import lax
from jax.experimental import pallas as pl
from jax.experimental.pallas import tpu as pltpu
from jax.sharding import PartitionSpec as P

REACH = 3
HALO = 2 * REACH
PACK = 8
NET = PACK - 2
OFF = -1e30
VMEM_LIMIT = 44 * 2**20
F32, BF16 = jnp.float32, jnp.bfloat16


def split(value):
    high = value.astype(BF16)
    return high, (value - high.astype(F32)).astype(BF16)


def silu_of_double(half):
    return half + half * jnp.tanh(half)


def lane_groups(shape, size):
    return lax.broadcasted_iota(jnp.int32, shape, len(shape) - 1) // size


def pack_kernel(start_ref, embed_ref, dx_ref, eps_ref, mid_ref, even_ref, odd_ref, par_ref):
    chans, rows, all_cols = start_ref.shape
    here, hid = embed_ref.shape
    first = lax.axis_index("tm") * (all_cols // lax.axis_size("tm")) - HALO
    shift = lax.rem(all_cols - first, all_cols)
    depth = mid_ref.shape[2]
    value = pltpu.roll(start_ref[...].reshape(chans * rows, all_cols), shift, 1)[:, :depth]
    place = lax.broadcasted_iota(jnp.int32, value.shape, 1) + first
    value = jnp.where((place >= 0) & (place < all_cols), value, 0.0)
    for c in range(chans):
        mid_ref[:, c, :] = value[c * rows : (c + 1) * rows]
    odd = lax.rem(lax.axis_index("space"), 2)
    even_ref[...] = mid_ref[pl.ds((1 - odd) * (rows - HALO), HALO)]
    odd_ref[...] = mid_ref[pl.ds(odd * (rows - HALO), HALO)]
    par_ref[:, :hid] = embed_ref[...]
    lane = lax.broadcasted_iota(jnp.int32, (1, hid), 1)
    for t in range(here):
        par_ref[t : t + 1, hid:] = jnp.where(
            lane == 0, dx_ref[t], jnp.where(lane == 1, eps_ref[t], 0.0)
        )


def weights_kernel(
    states, wi_ref, wm_ref, wo_ref, bi_ref, bm_ref, bo_ref,
    wi_out, wm_out, wo_out, wo_last, bias_out, sums_out,
):
    hid, chans = wi_ref.shape[2], wi_ref.shape[3]
    taps = [wi_ref[a, b] * 0.5 for a in range(3) for b in range(3)]
    first = jnp.concatenate(taps[:8], 1).T
    ninth = jnp.concatenate([taps[8]] * 8, 1).T
    taps = [first[t * chans : (t + 1) * chans] for t in range(8)] + [ninth[:chans]]
    terms = [split(jnp.concatenate(taps[3 * a : 3 * a + 3], 1)) for a in range(3)]
    high, low = [t[0] for t in terms], [t[1] for t in terms]
    none = jnp.zeros_like(high[0])
    upper = high + [none] + low + [none]
    lower = high + [none] * 5
    for r in range(NET):
        for g in range(PACK):
            at = (g + r) % PACK * chans
            wi_out[r, at : at + chans] = upper[g]
            wi_out[r, hid + at : hid + at + chans] = lower[g]
    for a in range(3):
        w0, w1, w2 = (wm_ref[a, b].T * 0.5 for b in range(3))
        even, odd = w0 * (1 / 24) + w2 * (1 / 6), w1 * (1 / 12)
        sides = (w0 + w2) * (-1 / 6)
        middle = w1 * (-1 / 6)
        forms = (w0 * 0.25, sides + middle, sides - middle, even + odd, even - odd, w2)
        for point, form in enumerate(forms):
            both = jnp.concatenate(split(form), 1)
            wm_out[point, 2 * a * hid : (2 * a + 1) * hid] = both
            wm_out[point, (2 * a + 1) * hid : (2 * a + 2) * hid] = both
    count = PACK + 2
    empty = jnp.zeros((chans, hid), F32)
    for k in range(count):
        for b in range(3):
            band = jnp.concatenate(
                [wo_ref[k - r, b] if 0 <= k - r < 3 else empty for r in range(PACK)], 0
            ).T
            high, low = split(band)
            if b < 2:
                lanes = slice(b * hid, (b + 1) * hid)
                wo_out[2 * k * hid : (2 * k + 1) * hid, lanes] = high
                wo_out[(2 * k + 1) * hid : (2 * k + 2) * hid, lanes] = high
                wo_out[(2 * count + k) * hid : (2 * count + k + 1) * hid, lanes] = low
            else:
                both = jnp.concatenate([high, low], 1)
                wo_last[2 * k * hid : (2 * k + 1) * hid] = both
                wo_last[(2 * k + 1) * hid : (2 * k + 2) * hid] = both
    bias_out[0:1] = bi_ref[...].reshape(1, hid) * 0.5
    bias_out[1:2] = bm_ref[...].reshape(1, hid) * 0.5
    bias_out[2:3] = jnp.concatenate([bo_ref[...].reshape(1, chans)] * PACK, 1)
    size = sums_out.shape[0]
    source = lax.broadcasted_iota(jnp.int32, (size, size), 0)
    target = lax.broadcasted_iota(jnp.int32, (size, size), 1)
    cols = size // states
    same = (source // states) == (target % cols)
    upto = (source % states) <= (target // cols)
    sums_out[...] = jnp.where(same & upto, 1.0, 0.0).astype(BF16)


def main_kernel(tm, *refs):
    mid_ref, even_ref, odd_ref = refs[:3]
    pars = refs[3 : 3 + tm]
    bias_ref, wi_ref, wm_ref, wo_ref, wo_last, sums_ref = refs[3 + tm : 9 + tm]
    outs = refs[9 + tm : 9 + 2 * tm]
    (
        rows_s, par_s, held_s, start_s, common_s, points_s, hid2_s, inputs_s, chunk_s,
        in_bias, mid_bias, eps_s,
    ) = refs[9 + 2 * tm :]
    rows, chans, depth = mid_ref.shape
    states, hid = par_s.shape[0], par_s.shape[1] // 2
    groups = points_s.shape[2] // states
    wide = 4 * groups
    cols = wide - 8
    my_tm, my_space = lax.axis_index("tm"), lax.axis_index("space")
    all_rows, all_cols = rows * lax.axis_size("space"), cols * tm
    row0, col0 = my_space * rows, my_tm * cols

    here = states // tm
    for k in range(tm):
        held_s[k] = pars[k][...]
    for k in range(tm):
        par_s[k * here : (k + 1) * here] = held_s[my_tm ^ k]

    embed = par_s[:, :hid]
    drift_x = jnp.broadcast_to(par_s[:, hid : hid + 1], (states, hid))
    drift_eps = jnp.broadcast_to(par_s[:, hid + 1 : hid + 2], (states, hid))

    def inside(first, width, limit):
        place = lax.broadcasted_iota(jnp.int32, (width, states, hid), 0)
        return (place + first >= 0) & (place + first < all_cols) & (place < limit)

    bias = bias_ref[0:1] + 0.5 * embed
    in_bias[0] = jnp.full(in_bias.shape[1:], OFF, F32)
    in_bias[1] = jnp.where(inside(col0 - 5, wide + 4, wide + 2), bias[None], OFF)
    mid_bias[0] = jnp.full(mid_bias.shape[1:], OFF, F32)
    mid_bias[1] = jnp.where(
        inside(col0 - 4, wide + 3, wide + 3),
        jnp.broadcast_to(bias_ref[1:2], (states, hid))[None],
        OFF,
    )
    reach_cols = cols + HALO
    eps_s[...] = jnp.where(inside(col0 - 3, reach_cols, reach_cols), drift_eps[None], 0.0)
    out_bias = bias_ref[2:3]

    def in_field(row):
        return jnp.where((row >= 0) & (row < all_rows), 1, 0)

    odd = lax.rem(my_space, 2) == 1
    rows_s[:HALO] = jnp.where(odd, even_ref[...], odd_ref[...])
    rows_s[HALO : HALO + rows] = mid_ref[...]
    rows_s[HALO + rows :] = jnp.where(odd, odd_ref[...], even_ref[...])

    def packed_start(first):
        return rows_s[first : first + PACK].reshape(PACK * chans, depth).T

    def first_conv(r, values):
        group = lane_groups(values[0].shape, chans)
        own = (group >= r) & (group <= r + 2)
        left = []
        for value in values:
            turned = pltpu.roll(value, hid // 2, 1)
            low = split(value)[1]
            left.append(jnp.concatenate([jnp.where(own, value, turned).astype(BF16), low], 1))
        return jnp.dot(jnp.concatenate(left, 0), wi_ref[r], preferred_element_type=F32)

    def to_points(row, field):
        fours = field.reshape(groups + 1, 4, states, hid)
        d0, d1, d2, d3 = (fours[:groups, k] for k in range(4))
        d4, d5 = fours[1:, 0], fours[1:, 1]
        e1, e2 = d4 - 4 * d2, d3 - 4 * d1
        e3, e4 = d4 - d2, 2 * (d3 - d1)
        forms = (4 * (d0 - d2) + e3, e1 + e2, e1 - e2, e3 + e4, e3 - e4, (d5 - d3) - 2 * e4)
        for point, form in enumerate(forms):
            high, low = split(form.reshape(groups * states, hid))
            points_s[point, row, :, :hid] = high
            points_s[point, row, :, hid:] = low

    def second_hidden(count, step, row_first, col_first):
        def body(c, _):
            first = c * step
            sums = []
            for point in range(6):
                left = jnp.concatenate(
                    [
                        points_s[point, pl.ds(first + a, step)].reshape(step * groups * states, 2 * hid)
                        for a in range(3)
                    ],
                    1,
                )
                both = jnp.dot(left, wm_ref[point], preferred_element_type=F32)
                sums.append((both[:, :hid] + both[:, hid:]).reshape(step, groups, states, hid))
            m0, m1, m2, m3, m4, m5 = sums
            s1, t1, s3, t3 = m1 + m2, m1 - m2, m3 + m4, m3 - m4
            field = jnp.stack(
                [m0 + s1 + s3, t1 + 2 * t3, s1 + 4 * s3, t1 + 8 * t3 + m5], 2
            ).reshape(step, wide, states, hid)
            for r in range(step):
                ok = in_field(row0 + row_first + first + r)
                value = silu_of_double(field[r] + mid_bias[ok, col_first : col_first + wide])
                high, low = split(value.reshape(wide * states, hid))
                hid2_s[first + r, :, :hid] = high
                hid2_s[first + r, :, hid:] = low
            return 0

        lax.fori_loop(0, count // step, body, 0)

    def noise(packs, width):
        count = PACK + 2
        both = [
            jnp.concatenate([hid2_s[NET * p + k] for p in range(packs)], 0) for k in range(count)
        ]
        left = jnp.concatenate(both + [v[:, :hid] for v in both], 1)
        two = jnp.dot(left, wo_ref[...], preferred_element_type=F32)
        last = jnp.dot(left[:, : 2 * count * hid], wo_last[...], preferred_element_type=F32)
        shape = (packs, wide, states, hid)
        t0, t1 = two[:, :hid].reshape(shape), two[:, hid:].reshape(shape)
        t2 = (last[:, :hid] + last[:, hid:]).reshape(shape)
        return t0[:, :width] + t1[:, 1 : width + 1] + t2[:, 2 : width + 2] + out_bias

    state = lax.broadcasted_iota(jnp.int32, (1, states, hid), 1)

    def earlier(value):
        value = jnp.where(state >= 1, pltpu.roll(value, 1, 1), 0.0)
        reach = 1
        while reach < states:
            value = value + jnp.where(state >= reach, pltpu.roll(value, reach, 1), 0.0)
            reach *= 2
        return value

    packs = start_s.shape[0]
    for p in range(packs):
        start_s[p] = packed_start(NET * p)

    def first_rows(r, _):
        taps = first_conv(r, [start_s[p] for p in range(packs)])
        for p in range(packs):
            t0, t1, t2 = (
                taps[p * depth : (p + 1) * depth, k * hid : (k + 1) * hid] for k in range(3)
            )
            common_s[NET * p + r] = t0 + pltpu.roll(t1, depth - 1, 0) + pltpu.roll(t2, depth - 2, 0)
        return 0

    lax.fori_loop(0, NET, first_rows, 0)

    def first_points(i, _):
        ok = in_field(row0 - 5 + i)
        to_points(i, silu_of_double(common_s[i, : wide + 4][:, None, :] + in_bias[ok]))
        return 0

    lax.fori_loop(0, rows + 10, first_points, 0)
    second_hidden(rows + 8, 4, -4, 0)

    packs = inputs_s.shape[0]
    value = noise(packs, reach_cols)
    group = lane_groups((1, hid), chans)
    for p in range(packs):
        start = packed_start(REACH + NET * p)[REACH : REACH + reach_cols]
        start = jnp.broadcast_to(start[:, None, :], (reach_cols, states, hid))
        row = group + (row0 - REACH + NET * p)
        keep = jnp.where((row >= 0) & (row < all_rows), 1.0, 0.0)
        drift = drift_x[None] * start + eps_s[...] * (value[p] * keep)
        total = (start + earlier(drift)).reshape(reach_cols * states, hid)
        inputs_s[p, : reach_cols * states] = total
        inputs_s[p, reach_cols * states :] = jnp.zeros(((wide - reach_cols) * states, hid), F32)

    def second_rows(r, _):
        taps = first_conv(r, [inputs_s[p] for p in range(packs)])
        width = cols + 4
        for p in range(packs):
            first = p * wide * states
            t0, t1, t2 = (
                taps[first + k * states : first + (k + width) * states, k * hid : (k + 1) * hid]
                for k in range(3)
            )
            i = NET * p + r
            ok = in_field(row0 - 2 + i)
            value = (t0 + t1 + t2).reshape(width, states, hid) + in_bias[ok, 3 : 3 + width]
            value = silu_of_double(value)
            to_points(i, jnp.concatenate([value, jnp.zeros((8, states, hid), F32)], 0))
        return 0

    lax.fori_loop(0, NET, second_rows, 0)
    second_hidden(rows + 2, 5, -1, 3)

    value = noise(1, cols)[0]
    size = cols * states
    upper = inputs_s[0, REACH * states : REACH * states + size]
    lower = inputs_s[1, REACH * states : REACH * states + size]
    inputs = jnp.where(
        lane_groups((size, hid), chans) < PACK - REACH,
        pltpu.roll(upper, hid - REACH * chans, 1),
        pltpu.roll(lower, (NET - REACH) * chans, 1),
    ).reshape(cols, states, hid)
    drift = drift_x[None] * inputs + drift_eps[None] * value
    high, low = split(drift.reshape(size, hid).T)
    total = jnp.dot(high, sums_ref[...], preferred_element_type=F32) + jnp.dot(
        low, sums_ref[...], preferred_element_type=F32
    )
    start = mid_ref[...].reshape(rows * chans, depth)[:, HALO : HALO + cols]
    start = jnp.concatenate([start] * here, 1)
    width = here * cols
    for k in range(tm):
        value = start + total[:, k * width : (k + 1) * width]
        for r in range(rows):
            chunk_s[k, :, r, :] = value[r * chans : (r + 1) * chans]
    for k in range(tm):
        outs[k][...] = chunk_s[my_tm ^ k]


def join_kernel(tm, *refs):
    blocks, out_ref, held = refs[:tm], refs[tm], refs[tm + 1]
    here = out_ref.shape[0]
    cols = out_ref.shape[3] // tm
    for k in range(tm):
        held[k] = blocks[k][...]
    my_tm = lax.axis_index("tm")
    for k in range(tm):
        block = held[my_tm ^ k]
        for t in range(here):
            out_ref[t, :, :, k * cols : (k + 1) * cols] = block[:, :, t * cols : (t + 1) * cols]


def kernel_call(body, out_shape, in_specs, scratch=(), flops=0, read=0):
    vmem = pl.BlockSpec(memory_space=pltpu.VMEM)
    if isinstance(in_specs, int):
        in_specs = [vmem] * in_specs
    return pl.pallas_call(
        body,
        out_shape=out_shape,
        in_specs=in_specs,
        out_specs=jax.tree.map(lambda _: vmem, out_shape),
        scratch_shapes=list(scratch),
        compiler_params=pltpu.CompilerParams(vmem_limit_bytes=VMEM_LIMIT),
        cost_estimate=pl.CostEstimate(flops=flops, bytes_accessed=read, transcendentals=0),
    )


def on_device(start_latent, time_embed, drift_x, drift_eps, w_in, b_in, w_mid, b_mid, w_out, b_out):
    tm, space = lax.axis_size("tm"), lax.axis_size("space")
    chans, rows, all_cols = start_latent.shape
    here, hid = time_embed.shape
    states, cols = here * tm, all_cols // tm
    depth = -(-(cols + 2 * HALO) // 128) * 128
    assert rows == PACK and hid == PACK * chans
    shape = jax.ShapeDtypeStruct
    vmem, smem = (pl.BlockSpec(memory_space=m) for m in (pltpu.VMEM, pltpu.SMEM))

    edge = shape((HALO, chans, depth), F32)
    mid, even, odd, par = kernel_call(
        pack_kernel,
        (shape((rows, chans, depth), F32), edge, edge, shape((here, 2 * hid), F32)),
        [vmem, vmem, smem, smem],
        read=10**6,
    )(start_latent, time_embed, drift_x, drift_eps)
    even = lax.ppermute(even, "space", [(i, i ^ 1) for i in range(space) if i ^ 1 < space])
    pairs = [(i, i + 1) for i in range(1, space - 1, 2)]
    odd = lax.ppermute(odd, "space", pairs + [(b, a) for a, b in pairs])
    pars = [par] + [
        lax.ppermute(par, "tm", [(i, i ^ k) for i in range(tm)]) for k in range(1, tm)
    ]

    taps = (PACK + 2) * hid
    weights = kernel_call(
        functools.partial(weights_kernel, states),
        (
            shape((NET, 2 * hid, 3 * hid), BF16),
            shape((6, 6 * hid, 2 * hid), BF16),
            shape((3 * taps, 2 * hid), BF16),
            shape((2 * taps, 2 * hid), BF16),
            shape((8, hid), F32),
            shape((cols * states, cols * states), BF16),
        ),
        6,
        flops=10**7,
        read=8 * 10**6,
    )(w_in, w_mid, w_out, b_in, b_mid, b_out)
    wi, wm, wo, wo_last, bias, sums = weights

    groups = (cols + 8) // 4
    wide = 4 * groups
    width = here * cols
    chunks = kernel_call(
        functools.partial(main_kernel, tm),
        tuple(shape((chans, rows, width), F32) for _ in range(tm)),
        9 + tm,
        scratch=(
            pltpu.VMEM((rows + 2 * HALO, chans, depth), F32),
            pltpu.VMEM((states, 2 * hid), F32),
            pltpu.VMEM((tm, here, 2 * hid), F32),
            pltpu.VMEM(((rows + 2 * HALO - 2) // NET, depth, hid), F32),
            pltpu.VMEM((rows + 10, depth, hid), F32),
            pltpu.VMEM((6, rows + 10, groups * states, 2 * hid), BF16),
            pltpu.VMEM((rows + 8, wide * states, 2 * hid), BF16),
            pltpu.VMEM(((rows + HALO - 2) // NET, wide * states, hid), F32),
            pltpu.VMEM((tm, chans, rows, width), F32),
            pltpu.VMEM((2, wide + 4, states, hid), F32),
            pltpu.VMEM((2, wide + 3, states, hid), F32),
            pltpu.VMEM((cols + HALO, states, hid), F32),
        ),
        flops=10**10,
        read=8 * 10**6,
    )(mid, even, odd, *pars, bias, wi, wm, wo, wo_last, sums)

    blocks = [chunks[0]] + [
        lax.ppermute(chunks[k], "tm", [(i, i ^ k) for i in range(tm)]) for k in range(1, tm)
    ]
    return kernel_call(
        functools.partial(join_kernel, tm),
        shape((here, chans, rows, all_cols), F32),
        tm,
        scratch=(pltpu.VMEM((tm, chans, rows, width), F32),),
        read=10**6,
    )(*blocks)


def solution(mesh):
    in_specs = (
        P("group", "space", None),
        P("tm", None),
        P("tm"),
        P("tm"),
        P(),
        P(),
        P(),
        P(),
        P(),
        P(),
    )
    out_specs = P("tm", "group", "space", None)
    return jax.shard_map(
        on_device, mesh=mesh, in_specs=in_specs, out_specs=out_specs, check_vma=False
    )
```

time: 79.8 us -> 52.8 us (0.66)
  Pallas kernels: 50.8 us -> 31.4 us
  blocking collectives: 6.18 us -> 0 us
  starting transfers between devices: 7.42 us -> 9.62 us
  other arithmetic: 1.55 us -> 0 us
  local copies, waits for them, and re-layouts: 9.29 us -> 7.91 us
    pallas_call x1, Pallas kernels: 46 us -> 28.4 us  [on_device(): kernel_call(functools.partial(main_kernel, tm), tuple((shape((chans, rows...]
    all_gather x1 -> x0, blocking collectives: 6.18 us -> none  [on_device(): par = lax.all_gather(par, 'tm', tiled=True)]
    unnamed x15 -> x19, local copies, waits for them, and re-layouts: 3.41 us -> 7.91 us
    another operation x3 -> x0, local copies, waits for them, and re-layouts: 2.21 us -> none  [on_device(): bias = jnp.stack([b_in, b_mid, jnp.tile(b_out, hid // chans)] + [b_in] * 5)]
    ppermute x2 -> x5, starting transfers between devices: 5.28 us -> 7.42 us  [the longest x1 4.48 us: on_device(): odd = lax.ppermute(odd, 'space', pairs + [(b, a) for a, b in pairs])]
    broadcast_in_dim x4 -> x0, local copies, waits for them, and re-layouts: 1.49 us -> none  [the longest x1 0.74 us: on_device(): drift_x[:, None]]
    transpose x2 -> x0, local copies, waits for them, and re-layouts: 1.01 us -> none  [the longest x1 0.92 us: on_device(): wi = w_in.transpose(0, 3, 1, 2).reshape(3 * chans, 3 * hid)]
    reshape x1 -> x0, local copies, waits for them, and re-layouts: 1.01 us -> none  [on_device(): wo = w_out.transpose(0, 3, 1, 2).reshape(3, hid, 3 * chans)]
  transfers between devices with their start and end apart: 5 -> 8, of which waited for: 2 -> 2; matrix products, arithmetic and copies ran while one was open for 11% -> 2% of each run, Pallas kernels for 4% -> 3%
where the time goes in v1:
time: 52.8 us; the launch traced here: 52.5 us
  Pallas kernels  31.4 us (59%)
  starting transfers between devices  9.62 us (18%)
  local copies, waits for them, and re-layouts  7.91 us (15%)
  waiting for transfers between devices  3.45 us (7%)
    pallas_call x1, Pallas kernels, on_device(): kernel_call(functools.partial(main_kernel, tm), tuple((shape((chans, rows...  28.4 us
    unnamed x19, local copies, waits for them, and re-layouts  7.91 us
    ppermute x1, starting transfers between devices, on_device(): odd = lax.ppermute(odd, 'space', pairs + [(b, a) for a, b in pairs])  4.48 us
    ppermute x3, waiting for transfers between devices, on_device(): lax.ppermute(chunks[k], 'tm', [(i, i ^ k) for i in range(tm)])  3.43 us
    ppermute x3, starting transfers between devices, on_device(): lax.ppermute(par, 'tm', [(i, i ^ k) for i in range(tm)])  2.87 us
    ppermute x3, starting transfers between devices, on_device(): lax.ppermute(chunks[k], 'tm', [(i, i ^ k) for i in range(tm)])  2.21 us
    pallas_call x1, Pallas kernels, on_device(): kernel_call(functools.partial(weights_kernel, states), (shape((NET, 2 * h...  1.39 us
  transfers between devices with their start and end apart: 8, of which 2 were waited for; matrix products, arithmetic and copies ran while one was open for 2% of the time, Pallas kernels for 3%

profile of v1, /device:TPU:9, one launch (start us, length us, event | category | flops | bytes accessed | tf_op | source)
XLA Modules:
  0.0 52.5 jit_solution(1838630766207745658)
XLA Ops:
  0.0 0.0 copy-start.1
  0.0 0.9 %copy-done.1 = f32[16,8,256]{2,1,0:T(8,128)S(1)} copy-done((f32[16,8,256]{2,1,0:T(8,128)S(1)}, f32[16,8,256]{2,1,0:T(8,128)}, u32[]{:S(2)}) %copy-start.1) | copy-done | bytes 131096
  0.9 0.0 copy-start.3
  0.9 0.7 %copy-done.3 = f32[2,128]{1,0:T(2,128)S(1)} copy-done((f32[2,128]{1,0:T(2,128)S(1)}, f32[2,128]{1,0:T(2,128)}, u32[]{:S(2)}) %copy-start.3) | copy-done | bytes 1048
  1.6 0.0 copy-start.4
  1.6 0.7 %copy-done.4 = f32[2]{0:T(128)S(1)} copy-done((f32[2]{0:T(128)S(1)}, f32[2]{0:T(128)}, u32[]{:S(2)}) %copy-start.4) | copy-done | bytes 32
  2.2 0.0 copy-start.5
  2.2 0.7 %copy-done.5 = f32[2]{0:T(128)S(1)} copy-done((f32[2]{0:T(128)S(1)}, f32[2]{0:T(128)}, u32[]{:S(2)}) %copy-start.5) | copy-done | bytes 32
  2.9 0.7 %shard_map.100 = (f32[8,16,128]{2,1,0:T(8,128)S(1)}, f32[6,16,128]{2,1,0:T(8,128)S(1)}, f32[6,16,128]{2,1,0:T(8,128)S(1)}, f32[2,256]{1,0:T(2,128)S(1)}) custom-call(f32[16,8,256]{2,1,0:T(8,128)S(1)} %copy-done.1, f32[2,128]{1,0:T(2,128)S(1)} %copy-done.3, f32[2]{0:T(128)S(1)} %copy-done.4, f32[2]{0:T(128)S(1)} %copy-done.5), custom_call_target="tpu_custom_call" | custom-call | bytes 1000000 | tf_op jit(solution)/shard_map/pallas_call | solution.py:360
  3.6 0.1 collective-permute-start
  3.7 4.5 %collective-permute-start.1 = (f32[6,16,128]{2,1,0:T(8,128)S(1)}, f32[6,16,128]{2,1,0:T(8,128)S(1)}, u32[]{:S(2)}, u32[]{:S(2)}) collective-permute-start(f32[6,16,128]{2,1,0:T(8,128)S(1)} %get-tuple-element.21), channel_id=1, source_target_pairs={{1,2},{2,1},{5,6},{6,5},{9,10},{10,9},{13,14},{14,13},{17,18},{18,... | collective-permute-start | bytes 147464 | tf_op jit(solution)/shard_map/ppermute | solution.py:368
  8.2 2.4 %collective-permute-start.4 = (f32[2,256]{1,0:T(2,128)S(1)}, f32[2,256]{1,0:T(2,128)S(1)}, u32[]{:S(2)}, u32[]{:S(2)}) collective-permute-start(f32[2,256]{1,0:T(2,128)S(1)} %get-tuple-element.22.refs_3_), channel_id=1, source_target_pairs={{0,12},{4,8},{8,4},{12,0},{1,13},{5,9},{9,5},{13,1},{2,14},{6,10},... | collective-permute-start | bytes 6152 | tf_op jit(solution)/shard_map/ppermute | solution.py:370
  10.6 0.3 collective-permute-start.3
  10.8 0.2 collective-permute-start.2
  11.0 1.1 %copy.11.wi_ref = f32[3,3,128,16]{3,2,1,0:T(8,128)S(1)} copy(f32[3,3,128,16]{2,3,1,0:T(8,128)} %param.14) | data formatting | bytes 147456 | tf_op args[4]
  12.2 0.0 copy-start
  12.2 1.1 %copy-done = f32[3,3,128,128]{3,2,1,0:T(8,128)S(1)} copy-done((f32[3,3,128,128]{3,2,1,0:T(8,128)S(1)}, f32[3,3,128,128]{3,2,1,0:T(8,128)}, u32[]{:S(2)}) %copy-start) | copy-done | bytes 589848
  13.2 0.0 copy-start.2
  13.2 0.9 %copy-done.2 = f32[3,3,16,128]{3,2,1,0:T(8,128)S(1)} copy-done((f32[3,3,16,128]{3,2,1,0:T(8,128)S(1)}, f32[3,3,16,128]{3,2,1,0:T(8,128)}, u32[]{:S(2)}) %copy-start.2) | copy-done | bytes 73752
  14.1 0.0 copy-start.6
  14.1 0.7 %copy-done.6 = f32[128]{0:T(128)S(1)} copy-done((f32[128]{0:T(128)S(1)}, f32[128]{0:T(128)}, u32[]{:S(2)}) %copy-start.6) | copy-done | bytes 536
  14.8 0.0 copy-start.7
  14.8 0.7 %copy-done.7 = f32[128]{0:T(128)S(1)} copy-done((f32[128]{0:T(128)S(1)}, f32[128]{0:T(128)}, u32[]{:S(2)}) %copy-start.7) | copy-done | bytes 536
  15.4 0.0 copy-start.8
  15.4 0.7 %copy-done.8 = f32[16]{0:T(128)S(1)} copy-done((f32[16]{0:T(128)S(1)}, f32[16]{0:T(128)}, u32[]{:S(2)}) %copy-start.8) | copy-done | bytes 88
  16.1 1.4 %shard_map.101 = (bf16[6,256,384]{2,1,0:T(8,128)(2,1)S(1)}, bf16[6,768,256]{2,1,0:T(8,128)(2,1)S(1)}, bf16[3840,256]{1,0:T(8,128)(2,1)S(1)}, bf16[2560,256]{1,0:...) custom-call(f32[3,3,128,16]{3,2,1,0:T(8,128)S(1)} %copy.11.wi_ref, f32[3,3,128,128]{3,2,1,0:T(8,128)S(1)} %copy-done, ...), custom_call_target="tpu_custom_call" | custom-call | flops 10000000 | bytes 8000000 | tf_op jit(solution)/shard_map/pallas_call | solution.py:374
  17.5 0.0 collective-permute-done.4.refs_6_
  17.5 0.0 collective-permute-done.3.refs_5_
  17.5 0.0 collective-permute-done.2.refs_4_
  17.5 0.0 collective-permute-done.refs_1_
  17.5 0.0 collective-permute-done.1.refs_2_
  17.5 28.4 %shard_map.102 = (f32[16,8,128]{2,1,0:T(8,128)S(1)}, f32[16,8,128]{2,1,0:T(8,128)S(1)}, f32[16,8,128]{2,1,0:T(8,128)S(1)}, f32[16,8,128]{2,1,0:T(8,128)S(1)}) custom-call(f32[8,16,128]{2,1,0:T(8,128)S(1)} %get-tuple-element.19.refs_0_, f32[6,16,128]{2,1,0:T(8,128)S(1)} %collective-permute-done.refs_1_, f32[6,16,128]{2,1,0:T(8,128)S(1)} %collective-permute-done.1.refs_2_, ...), custom_call_target="tpu_custom_call" | custom-call | flops 10000000000 | bytes 8000000 | tf_op jit(solution)/shard_map/pallas_call | solution.py:393
  46.0 0.3 collective-permute-start.5
  46.3 1.3 %collective-permute-start.6 = (f32[16,8,128]{2,1,0:T(8,128)S(1)}, f32[16,8,128]{2,1,0:T(8,128)S(1)}, u32[]{:S(2)}, u32[]{:S(2)}) collective-permute-start(f32[16,8,128]{2,1,0:T(8,128)S(1)} %get-tuple-element.31), channel_id=1, source_target_pairs={{0,8},{4,12},{8,0},{12,4},{1,9},{5,13},{9,1},{13,5},{2,10},{6,14},... | collective-permute-start | bytes 196616 | tf_op jit(solution)/shard_map/ppermute | solution.py:416
  47.5 0.6 %collective-permute-start.7 = (f32[16,8,128]{2,1,0:T(8,128)S(1)}, f32[16,8,128]{2,1,0:T(8,128)S(1)}, u32[]{:S(2)}, u32[]{:S(2)}) collective-permute-start(f32[16,8,128]{2,1,0:T(8,128)S(1)} %get-tuple-element.32), channel_id=1, source_target_pairs={{0,12},{4,8},{8,4},{12,0},{1,13},{5,9},{9,5},{13,1},{2,14},{6,10},... | collective-permute-start | bytes 196616 | tf_op jit(solution)/shard_map/ppermute | solution.py:416
  48.2 0.0 collective-permute-done.5.refs_1_
  48.2 1.2 %collective-permute-done.6.refs_2_ = f32[16,8,128]{2,1,0:T(8,128)S(1)} collective-permute-done((f32[16,8,128]{2,1,0:T(8,128)S(1)}, f32[16,8,128]{2,1,0:T(8,128)S(1)}, u32[]{:S(2)}, u32[]{:S(2)}) %collective-permute-start.6) | collective-permute-done | bytes 65568 | tf_op jit(solution)/shard_map/ppermute | solution.py:416
  49.4 2.2 %collective-permute-done.7.refs_3_ = f32[16,8,128]{2,1,0:T(8,128)S(1)} collective-permute-done((f32[16,8,128]{2,1,0:T(8,128)S(1)}, f32[16,8,128]{2,1,0:T(8,128)S(1)}, u32[]{:S(2)}, u32[]{:S(2)}) %collective-permute-start.7) | collective-permute-done | bytes 65568 | tf_op jit(solution)/shard_map/ppermute | solution.py:416
  51.6 0.9 %shard_map.103 = f32[2,16,8,256]{3,2,1,0:T(8,128)} custom-call(f32[16,8,128]{2,1,0:T(8,128)S(1)} %get-tuple-element.29.refs_0_, f32[16,8,128]{2,1,0:T(8,128)S(1)} %collective-permute-done.5.refs_1_, f32[16,8,128]{2,1,0:T(8,128)S(1)} %collective-permute-done.6.refs_2_, f32[16,8,128]{2,1,0:T(8,128)S(1)} %collective-permute-done.7.refs_3_), custom_call_target="tpu_custom_call" | custom-call | bytes 1000000 | tf_op jit(solution)/shard_map/pallas_call | solution.py:418
Async XLA Ops:
  0.0 0.9 %copy-start.1 = (f32[16,8,256]{2,1,0:T(8,128)S(1)}, f32[16,8,256]{2,1,0:T(8,128)}, u32[]{:S(2)}) copy-start(f32[16,8,256]{2,1,0:T(8,128)} %start_ref.1) | copy-start | bytes 393220
  0.9 0.7 %copy-start.3 = (f32[2,128]{1,0:T(2,128)S(1)}, f32[2,128]{1,0:T(2,128)}, u32[]{:S(2)}) copy-start(f32[2,128]{1,0:T(2,128)} %embed_ref.1) | copy-start | bytes 3076
  1.6 0.7 %copy-start.4 = (f32[2]{0:T(128)S(1)}, f32[2]{0:T(128)}, u32[]{:S(2)}) copy-start(f32[2]{0:T(128)} %dx_ref.1) | copy-start | bytes 28
  2.2 0.7 %copy-start.5 = (f32[2]{0:T(128)S(1)}, f32[2]{0:T(128)}, u32[]{:S(2)}) copy-start(f32[2]{0:T(128)} %eps_ref.1) | copy-start | bytes 28
  3.6 13.9 %collective-permute-start = (f32[6,16,128]{2,1,0:T(8,128)S(1)}, f32[6,16,128]{2,1,0:T(8,128)S(1)}, u32[]{:S(2)}, u32[]{:S(2)}) collective-permute-start(f32[6,16,128]{2,1,0:T(8,128)S(1)} %get-tuple-element.20), channel_id=1, source_target_pairs={{0,1},{1,0},{2,3},{3,2},{4,5},{5,4},{6,7},{7,6},{8,9},{9,8},{10,11... | collective-permute-start | bytes 147464 | tf_op jit(solution)/shard_map/ppermute | solution.py:366
  3.7 13.8 %collective-permute-start.1 = (f32[6,16,128]{2,1,0:T(8,128)S(1)}, f32[6,16,128]{2,1,0:T(8,128)S(1)}, u32[]{:S(2)}, u32[]{:S(2)}) collective-permute-start(f32[6,16,128]{2,1,0:T(8,128)S(1)} %get-tuple-element.21), channel_id=1, source_target_pairs={{1,2},{2,1},{5,6},{6,5},{9,10},{10,9},{13,14},{14,13},{17,18},{18,... | collective-permute-start | bytes 147464 | tf_op jit(solution)/shard_map/ppermute | solution.py:368
  8.2 9.3 %collective-permute-start.4 = (f32[2,256]{1,0:T(2,128)S(1)}, f32[2,256]{1,0:T(2,128)S(1)}, u32[]{:S(2)}, u32[]{:S(2)}) collective-permute-start(f32[2,256]{1,0:T(2,128)S(1)} %get-tuple-element.22.refs_3_), channel_id=1, source_target_pairs={{0,12},{4,8},{8,4},{12,0},{1,13},{5,9},{9,5},{13,1},{2,14},{6,10},... | collective-permute-start | bytes 6152 | tf_op jit(solution)/shard_map/ppermute | solution.py:370
  10.6 6.9 %collective-permute-start.3 = (f32[2,256]{1,0:T(2,128)S(1)}, f32[2,256]{1,0:T(2,128)S(1)}, u32[]{:S(2)}, u32[]{:S(2)}) collective-permute-start(f32[2,256]{1,0:T(2,128)S(1)} %get-tuple-element.22.refs_3_), channel_id=1, source_target_pairs={{0,8},{4,12},{8,0},{12,4},{1,9},{5,13},{9,1},{13,5},{2,10},{6,14},... | collective-permute-start | bytes 6152 | tf_op jit(solution)/shard_map/ppermute | solution.py:370
  10.8 6.7 %collective-permute-start.2 = (f32[2,256]{1,0:T(2,128)S(1)}, f32[2,256]{1,0:T(2,128)S(1)}, u32[]{:S(2)}, u32[]{:S(2)}) collective-permute-start(f32[2,256]{1,0:T(2,128)S(1)} %get-tuple-element.22.refs_3_), channel_id=1, source_target_pairs={{0,4},{4,0},{8,12},{12,8},{1,5},{5,1},{9,13},{13,9},{2,6},{6,2},{1... | collective-permute-start | bytes 6152 | tf_op jit(solution)/shard_map/ppermute | solution.py:370
  12.2 1.1 %copy-start = (f32[3,3,128,128]{3,2,1,0:T(8,128)S(1)}, f32[3,3,128,128]{3,2,1,0:T(8,128)}, u32[]{:S(2)}) copy-start(f32[3,3,128,128]{3,2,1,0:T(8,128)} %wm_ref.1) | copy-start | bytes 1769476
  13.2 0.9 %copy-start.2 = (f32[3,3,16,128]{3,2,1,0:T(8,128)S(1)}, f32[3,3,16,128]{3,2,1,0:T(8,128)}, u32[]{:S(2)}) copy-start(f32[3,3,16,128]{3,2,1,0:T(8,128)} %wo_ref.1) | copy-start | bytes 221188
  14.1 0.7 %copy-start.6 = (f32[128]{0:T(128)S(1)}, f32[128]{0:T(128)}, u32[]{:S(2)}) copy-start(f32[128]{0:T(128)} %bi_ref.1) | copy-start | bytes 1540
  14.8 0.7 %copy-start.7 = (f32[128]{0:T(128)S(1)}, f32[128]{0:T(128)}, u32[]{:S(2)}) copy-start(f32[128]{0:T(128)} %bm_ref.1) | copy-start | bytes 1540
  15.4 0.7 %copy-start.8 = (f32[16]{0:T(128)S(1)}, f32[16]{0:T(128)}, u32[]{:S(2)}) copy-start(f32[16]{0:T(128)} %bo_ref.1) | copy-start | bytes 196
  46.0 2.2 %collective-permute-start.5 = (f32[16,8,128]{2,1,0:T(8,128)S(1)}, f32[16,8,128]{2,1,0:T(8,128)S(1)}, u32[]{:S(2)}, u32[]{:S(2)}) collective-permute-start(f32[16,8,128]{2,1,0:T(8,128)S(1)} %get-tuple-element.30), channel_id=1, source_target_pairs={{0,4},{4,0},{8,12},{12,8},{1,5},{5,1},{9,13},{13,9},{2,6},{6,2},{1... | collective-permute-start | bytes 196616 | tf_op jit(solution)/shard_map/ppermute | solution.py:416
  46.3 3.1 %collective-permute-start.6 = (f32[16,8,128]{2,1,0:T(8,128)S(1)}, f32[16,8,128]{2,1,0:T(8,128)S(1)}, u32[]{:S(2)}, u32[]{:S(2)}) collective-permute-start(f32[16,8,128]{2,1,0:T(8,128)S(1)} %get-tuple-element.31), channel_id=1, source_target_pairs={{0,8},{4,12},{8,0},{12,4},{1,9},{5,13},{9,1},{13,5},{2,10},{6,14},... | collective-permute-start | bytes 196616 | tf_op jit(solution)/shard_map/ppermute | solution.py:416
  47.5 4.0 %collective-permute-start.7 = (f32[16,8,128]{2,1,0:T(8,128)S(1)}, f32[16,8,128]{2,1,0:T(8,128)S(1)}, u32[]{:S(2)}, u32[]{:S(2)}) collective-permute-start(f32[16,8,128]{2,1,0:T(8,128)S(1)} %get-tuple-element.32), channel_id=1, source_target_pairs={{0,12},{4,8},{8,4},{12,0},{1,13},{5,9},{9,5},{13,1},{2,14},{6,10},... | collective-permute-start | bytes 196616 | tf_op jit(solution)/shard_map/ppermute | solution.py:416

commit v2 on v1

--- a/solution.py
+++ b/solution.py
@@ -28,7 +28,25 @@
     return lax.broadcasted_iota(jnp.int32, shape, len(shape) - 1) // size
 
 
-def pack_kernel(start_ref, embed_ref, dx_ref, eps_ref, mid_ref, even_ref, odd_ref, par_ref):
+def fetch(sources, targets, sems):
+    copies = [
+        pltpu.make_async_copy(source, target, sems.at[k])
+        for k, (source, target) in enumerate(zip(sources, targets))
+    ]
+    for copy in copies:
+        copy.start()
+    return copies
+
+
+def arrive(copies):
+    for copy in copies:
+        copy.wait()
+
+
+def pack_kernel(*refs):
+    sources, (mid_ref, even_ref, odd_ref, par_ref) = refs[:4], refs[4:8]
+    start_ref, embed_ref, dx_ref, eps_ref = refs[8:12]
+    arrive(fetch(sources, refs[8:12], refs[12]))
     chans, rows, all_cols = start_ref.shape
     here, hid = embed_ref.shape
     first = lax.axis_index("tm") * (all_cols // lax.axis_size("tm")) - HALO
@@ -50,16 +68,12 @@
         )
 
 
-def weights_kernel(
-    states, wi_ref, wm_ref, wo_ref, bi_ref, bm_ref, bo_ref,
-    wi_out, wm_out, wo_out, wo_last, bias_out, sums_out,
-):
-    hid, chans = wi_ref.shape[2], wi_ref.shape[3]
-    taps = [wi_ref[a, b] * 0.5 for a in range(3) for b in range(3)]
-    first = jnp.concatenate(taps[:8], 1).T
-    ninth = jnp.concatenate([taps[8]] * 8, 1).T
-    taps = [first[t * chans : (t + 1) * chans] for t in range(8)] + [ninth[:chans]]
-    terms = [split(jnp.concatenate(taps[3 * a : 3 * a + 3], 1)) for a in range(3)]
+def weights_kernel(states, *refs):
+    wi_out, wm_out, wo_out, wo_last, bias_out, sums_out = refs[6:12]
+    wi_ref, wm_ref, wo_ref, bi_ref, bm_ref, bo_ref = refs[12:18]
+    arrive(fetch(refs[:6], refs[12:18], refs[18]))
+    chans, hid = wi_ref.shape[2], wi_ref.shape[3]
+    terms = [split(jnp.concatenate([wi_ref[a, b] * 0.5 for b in range(3)], 1)) for a in range(3)]
     high, low = [t[0] for t in terms], [t[1] for t in terms]
     none = jnp.zeros_like(high[0])
     upper = high + [none] + low + [none]
@@ -346,6 +360,10 @@
     )
 
 
+def in_hbm(value):
+    return pltpu.with_memory_space_constraint(value, pltpu.HBM)
+
+
 def on_device(start_latent, time_embed, drift_x, drift_eps, w_in, b_in, w_mid, b_mid, w_out, b_out):
     tm, space = lax.axis_size("tm"), lax.axis_size("space")
     chans, rows, all_cols = start_latent.shape
@@ -353,16 +371,23 @@
     states, cols = here * tm, all_cols // tm
     depth = -(-(cols + 2 * HALO) // 128) * 128
     assert rows == PACK and hid == PACK * chans
-    shape = jax.ShapeDtypeStruct
-    vmem, smem = (pl.BlockSpec(memory_space=m) for m in (pltpu.VMEM, pltpu.SMEM))
-
-    edge = shape((HALO, chans, depth), F32)
+    shape, local = jax.ShapeDtypeStruct, pltpu.VMEM
+    hbm = pl.BlockSpec(memory_space=pltpu.HBM)
+
+    edge = local((HALO, chans, depth), F32)
     mid, even, odd, par = kernel_call(
         pack_kernel,
-        (shape((rows, chans, depth), F32), edge, edge, shape((here, 2 * hid), F32)),
-        [vmem, vmem, smem, smem],
+        (local((rows, chans, depth), F32), edge, edge, local((here, 2 * hid), F32)),
+        [hbm] * 4,
+        scratch=(
+            pltpu.VMEM((chans, rows, all_cols), F32),
+            pltpu.VMEM((here, hid), F32),
+            pltpu.SMEM((here,), F32),
+            pltpu.SMEM((here,), F32),
+            pltpu.SemaphoreType.DMA((4,)),
+        ),
         read=10**6,
-    )(start_latent, time_embed, drift_x, drift_eps)
+    )(*map(in_hbm, (start_latent, time_embed, drift_x, drift_eps)))
     even = lax.ppermute(even, "space", [(i, i ^ 1) for i in range(space) if i ^ 1 < space])
     pairs = [(i, i + 1) for i in range(1, space - 1, 2)]
     odd = lax.ppermute(odd, "space", pairs + [(b, a) for a, b in pairs])
@@ -374,17 +399,26 @@
     weights = kernel_call(
         functools.partial(weights_kernel, states),
         (
-            shape((NET, 2 * hid, 3 * hid), BF16),
-            shape((6, 6 * hid, 2 * hid), BF16),
-            shape((3 * taps, 2 * hid), BF16),
-            shape((2 * taps, 2 * hid), BF16),
-            shape((8, hid), F32),
-            shape((cols * states, cols * states), BF16),
+            local((NET, 2 * hid, 3 * hid), BF16),
+            local((6, 6 * hid, 2 * hid), BF16),
+            local((3 * taps, 2 * hid), BF16),
+            local((2 * taps, 2 * hid), BF16),
+            local((8, hid), F32),
+            local((cols * states, cols * states), BF16),
         ),
-        6,
+        [hbm] * 6,
+        scratch=(
+            pltpu.VMEM((3, 3, chans, hid), F32),
+            pltpu.VMEM((3, 3, hid, hid), F32),
+            pltpu.VMEM((3, 3, chans, hid), F32),
+            pltpu.VMEM((hid,), F32),
+            pltpu.VMEM((hid,), F32),
+            pltpu.VMEM((chans,), F32),
+            pltpu.SemaphoreType.DMA((6,)),
+        ),
         flops=10**7,
         read=8 * 10**6,
-    )(w_in, w_mid, w_out, b_in, b_mid, b_out)
+    )(*map(in_hbm, (w_in.transpose(0, 1, 3, 2), w_mid, w_out, b_in, b_mid, b_out)))
     wi, wm, wo, wo_last, bias, sums = weights
 
     groups = (cols + 8) // 4
@@ -392,7 +426,7 @@
     width = here * cols
     chunks = kernel_call(
         functools.partial(main_kernel, tm),
-        tuple(shape((chans, rows, width), F32) for _ in range(tm)),
+        tuple(local((chans, rows, width), F32) for _ in range(tm)),
         9 + tm,
         scratch=(
             pltpu.VMEM((rows + 2 * HALO, chans, depth), F32),

time: 52.8 us -> 45.9 us (0.87)
  local copies, waits for them, and re-layouts: 7.91 us -> 0 us
  Pallas kernels: 31.4 us -> 32.6 us
    unnamed x19 -> x0, local copies, waits for them, and re-layouts: 7.91 us -> none
    pallas_call x3, Pallas kernels: 30.5 us -> 31.7 us  [the longest x1 28.4 us: on_device(): kernel_call(functools.partial(main_kernel, tm), tuple((local((chans, rows...]
  transfers between devices with their start and end apart: 8 -> 8, of which waited for: 2 -> 2; matrix products, arithmetic and copies ran while one was open for 2% -> 0% of each run, Pallas kernels for 3% -> 5%
where the time goes in v2:
time: 45.9 us; the launch traced here: 45.7 us
  Pallas kernels  32.6 us (71%)
  starting transfers between devices  9.62 us (21%)
  waiting for transfers between devices  3.44 us (7%)
    pallas_call x1, Pallas kernels, on_device(): kernel_call(functools.partial(main_kernel, tm), tuple((local((chans, rows...  28.4 us
    ppermute x1, starting transfers between devices, on_device(): odd = lax.ppermute(odd, 'space', pairs + [(b, a) for a, b in pairs])  4.48 us
    ppermute x3, waiting for transfers between devices, on_device(): lax.ppermute(chunks[k], 'tm', [(i, i ^ k) for i in range(tm)])  3.43 us
    ppermute x3, starting transfers between devices, on_device(): lax.ppermute(par, 'tm', [(i, i ^ k) for i in range(tm)])  2.87 us
    pallas_call x1, Pallas kernels, on_device(): kernel_call(functools.partial(weights_kernel, states), (local((NET, 2 * h...  2.22 us
    ppermute x3, starting transfers between devices, on_device(): lax.ppermute(chunks[k], 'tm', [(i, i ^ k) for i in range(tm)])  2.21 us
    pallas_call x1, Pallas kernels, on_device(): kernel_call(pack_kernel, (local((rows, chans, depth), F32), edge, edge, l...  1.12 us
  transfers between devices with their start and end apart: 8, of which 2 were waited for; matrix products, arithmetic and copies ran while one was open for 0% of the time, Pallas kernels for 5%

profile of v2, /device:TPU:9, one launch (start us, length us, event | category | flops | bytes accessed | tf_op | source)
XLA Modules:
  0.0 45.7 jit_solution(4688545717953924771)
XLA Ops:
  0.0 1.1 %shard_map.100 = (f32[8,16,128]{2,1,0:T(8,128)S(1)}, f32[6,16,128]{2,1,0:T(8,128)S(1)}, f32[6,16,128]{2,1,0:T(8,128)S(1)}, f32[2,256]{1,0:T(2,128)S(1)}) custom-call(f32[16,8,256]{2,1,0:T(8,128)} %refs_0_.1, f32[2,128]{1,0:T(2,128)} %refs_1_.2, f32[2]{0:T(128)} %refs_2_.2, f32[2]{0:T(128)} %refs_3_.2), custom_call_target="tpu_custom_call" | custom-call | bytes 1000000 | tf_op jit(solution)/shard_map/pallas_call | solution.py:378
  1.1 0.1 collective-permute-start
  1.2 4.5 %collective-permute-start.1 = (f32[6,16,128]{2,1,0:T(8,128)S(1)}, f32[6,16,128]{2,1,0:T(8,128)S(1)}, u32[]{:S(2)}, u32[]{:S(2)}) collective-permute-start(f32[6,16,128]{2,1,0:T(8,128)S(1)} %get-tuple-element.21), channel_id=1, source_target_pairs={{1,2},{2,1},{5,6},{6,5},{9,10},{10,9},{13,14},{14,13},{17,18},{18,... | collective-permute-start | bytes 147464 | tf_op jit(solution)/shard_map/ppermute | solution.py:393
  5.7 2.4 %collective-permute-start.4 = (f32[2,256]{1,0:T(2,128)S(1)}, f32[2,256]{1,0:T(2,128)S(1)}, u32[]{:S(2)}, u32[]{:S(2)}) collective-permute-start(f32[2,256]{1,0:T(2,128)S(1)} %get-tuple-element.22.refs_3_), channel_id=1, source_target_pairs={{0,12},{4,8},{8,4},{12,0},{1,13},{5,9},{9,5},{13,1},{2,14},{6,10},... | collective-permute-start | bytes 6152 | tf_op jit(solution)/shard_map/ppermute | solution.py:395
  8.1 0.3 collective-permute-start.3
  8.3 0.2 collective-permute-start.2
  8.6 2.2 %shard_map.101 = (bf16[6,256,384]{2,1,0:T(8,128)(2,1)S(1)}, bf16[6,768,256]{2,1,0:T(8,128)(2,1)S(1)}, bf16[3840,256]{1,0:T(8,128)(2,1)S(1)}, bf16[2560,256]{1,0:...) custom-call(f32[3,3,16,128]{3,2,1,0:T(8,128)} %bitcast.1, f32[3,3,128,128]{3,2,1,0:T(8,128)} %refs_1_.3, ...), custom_call_target="tpu_custom_call" | custom-call | flops 10000000 | bytes 8000000 | tf_op jit(solution)/shard_map/pallas_call | solution.py:399
  10.8 0.0 collective-permute-done.4.refs_6_
  10.8 0.0 collective-permute-done.3.refs_5_
  10.8 0.0 collective-permute-done.2.refs_4_
  10.8 0.0 collective-permute-done.refs_1_
  10.8 0.0 collective-permute-done.1.refs_2_
  10.8 28.4 %shard_map.102 = (f32[16,8,128]{2,1,0:T(8,128)S(1)}, f32[16,8,128]{2,1,0:T(8,128)S(1)}, f32[16,8,128]{2,1,0:T(8,128)S(1)}, f32[16,8,128]{2,1,0:T(8,128)S(1)}) custom-call(f32[8,16,128]{2,1,0:T(8,128)S(1)} %get-tuple-element.19.refs_0_, f32[6,16,128]{2,1,0:T(8,128)S(1)} %collective-permute-done.refs_1_, f32[6,16,128]{2,1,0:T(8,128)S(1)} %collective-permute-done.1.refs_2_, ...), custom_call_target="tpu_custom_call" | custom-call | flops 10000000000 | bytes 8000000 | tf_op jit(solution)/shard_map/pallas_call | solution.py:427
  39.2 0.4 collective-permute-start.5
  39.6 1.2 %collective-permute-start.6 = (f32[16,8,128]{2,1,0:T(8,128)S(1)}, f32[16,8,128]{2,1,0:T(8,128)S(1)}, u32[]{:S(2)}, u32[]{:S(2)}) collective-permute-start(f32[16,8,128]{2,1,0:T(8,128)S(1)} %get-tuple-element.31), channel_id=1, source_target_pairs={{0,8},{4,12},{8,0},{12,4},{1,9},{5,13},{9,1},{13,5},{2,10},{6,14},... | collective-permute-start | bytes 196616 | tf_op jit(solution)/shard_map/ppermute | solution.py:450
  40.8 0.6 %collective-permute-start.7 = (f32[16,8,128]{2,1,0:T(8,128)S(1)}, f32[16,8,128]{2,1,0:T(8,128)S(1)}, u32[]{:S(2)}, u32[]{:S(2)}) collective-permute-start(f32[16,8,128]{2,1,0:T(8,128)S(1)} %get-tuple-element.32), channel_id=1, source_target_pairs={{0,12},{4,8},{8,4},{12,0},{1,13},{5,9},{9,5},{13,1},{2,14},{6,10},... | collective-permute-start | bytes 196616 | tf_op jit(solution)/shard_map/ppermute | solution.py:450
  41.4 0.0 collective-permute-done.5.refs_1_
  41.4 1.7 %collective-permute-done.6.refs_2_ = f32[16,8,128]{2,1,0:T(8,128)S(1)} collective-permute-done((f32[16,8,128]{2,1,0:T(8,128)S(1)}, f32[16,8,128]{2,1,0:T(8,128)S(1)}, u32[]{:S(2)}, u32[]{:S(2)}) %collective-permute-start.6) | collective-permute-done | bytes 65568 | tf_op jit(solution)/shard_map/ppermute | solution.py:450
  43.2 1.7 %collective-permute-done.7.refs_3_ = f32[16,8,128]{2,1,0:T(8,128)S(1)} collective-permute-done((f32[16,8,128]{2,1,0:T(8,128)S(1)}, f32[16,8,128]{2,1,0:T(8,128)S(1)}, u32[]{:S(2)}, u32[]{:S(2)}) %collective-permute-start.7) | collective-permute-done | bytes 65568 | tf_op jit(solution)/shard_map/ppermute | solution.py:450
  44.8 0.9 %shard_map.103 = f32[2,16,8,256]{3,2,1,0:T(8,128)} custom-call(f32[16,8,128]{2,1,0:T(8,128)S(1)} %get-tuple-element.29.refs_0_, f32[16,8,128]{2,1,0:T(8,128)S(1)} %collective-permute-done.5.refs_1_, f32[16,8,128]{2,1,0:T(8,128)S(1)} %collective-permute-done.6.refs_2_, f32[16,8,128]{2,1,0:T(8,128)S(1)} %collective-permute-done.7.refs_3_), custom_call_target="tpu_custom_call" | custom-call | bytes 1000000 | tf_op jit(solution)/shard_map/pallas_call | solution.py:452
Async XLA Ops:
  1.1 9.7 %collective-permute-start = (f32[6,16,128]{2,1,0:T(8,128)S(1)}, f32[6,16,128]{2,1,0:T(8,128)S(1)}, u32[]{:S(2)}, u32[]{:S(2)}) collective-permute-start(f32[6,16,128]{2,1,0:T(8,128)S(1)} %get-tuple-element.20), channel_id=1, source_target_pairs={{0,1},{1,0},{2,3},{3,2},{4,5},{5,4},{6,7},{7,6},{8,9},{9,8},{10,11... | collective-permute-start | bytes 147464 | tf_op jit(solution)/shard_map/ppermute | solution.py:391
  1.2 9.6 %collective-permute-start.1 = (f32[6,16,128]{2,1,0:T(8,128)S(1)}, f32[6,16,128]{2,1,0:T(8,128)S(1)}, u32[]{:S(2)}, u32[]{:S(2)}) collective-permute-start(f32[6,16,128]{2,1,0:T(8,128)S(1)} %get-tuple-element.21), channel_id=1, source_target_pairs={{1,2},{2,1},{5,6},{6,5},{9,10},{10,9},{13,14},{14,13},{17,18},{18,... | collective-permute-start | bytes 147464 | tf_op jit(solution)/shard_map/ppermute | solution.py:393
  5.7 5.1 %collective-permute-start.4 = (f32[2,256]{1,0:T(2,128)S(1)}, f32[2,256]{1,0:T(2,128)S(1)}, u32[]{:S(2)}, u32[]{:S(2)}) collective-permute-start(f32[2,256]{1,0:T(2,128)S(1)} %get-tuple-element.22.refs_3_), channel_id=1, source_target_pairs={{0,12},{4,8},{8,4},{12,0},{1,13},{5,9},{9,5},{13,1},{2,14},{6,10},... | collective-permute-start | bytes 6152 | tf_op jit(solution)/shard_map/ppermute | solution.py:395
  8.1 2.7 %collective-permute-start.3 = (f32[2,256]{1,0:T(2,128)S(1)}, f32[2,256]{1,0:T(2,128)S(1)}, u32[]{:S(2)}, u32[]{:S(2)}) collective-permute-start(f32[2,256]{1,0:T(2,128)S(1)} %get-tuple-element.22.refs_3_), channel_id=1, source_target_pairs={{0,8},{4,12},{8,0},{12,4},{1,9},{5,13},{9,1},{13,5},{2,10},{6,14},... | collective-permute-start | bytes 6152 | tf_op jit(solution)/shard_map/ppermute | solution.py:395
  8.3 2.5 %collective-permute-start.2 = (f32[2,256]{1,0:T(2,128)S(1)}, f32[2,256]{1,0:T(2,128)S(1)}, u32[]{:S(2)}, u32[]{:S(2)}) collective-permute-start(f32[2,256]{1,0:T(2,128)S(1)} %get-tuple-element.22.refs_3_), channel_id=1, source_target_pairs={{0,4},{4,0},{8,12},{12,8},{1,5},{5,1},{9,13},{13,9},{2,6},{6,2},{1... | collective-permute-start | bytes 6152 | tf_op jit(solution)/shard_map/ppermute | solution.py:395
  39.2 2.2 %collective-permute-start.5 = (f32[16,8,128]{2,1,0:T(8,128)S(1)}, f32[16,8,128]{2,1,0:T(8,128)S(1)}, u32[]{:S(2)}, u32[]{:S(2)}) collective-permute-start(f32[16,8,128]{2,1,0:T(8,128)S(1)} %get-tuple-element.30), channel_id=1, source_target_pairs={{0,4},{4,0},{8,12},{12,8},{1,5},{5,1},{9,13},{13,9},{2,6},{6,2},{1... | collective-permute-start | bytes 196616 | tf_op jit(solution)/shard_map/ppermute | solution.py:450
  39.6 3.5 %collective-permute-start.6 = (f32[16,8,128]{2,1,0:T(8,128)S(1)}, f32[16,8,128]{2,1,0:T(8,128)S(1)}, u32[]{:S(2)}, u32[]{:S(2)}) collective-permute-start(f32[16,8,128]{2,1,0:T(8,128)S(1)} %get-tuple-element.31), channel_id=1, source_target_pairs={{0,8},{4,12},{8,0},{12,4},{1,9},{5,13},{9,1},{13,5},{2,10},{6,14},... | collective-permute-start | bytes 196616 | tf_op jit(solution)/shard_map/ppermute | solution.py:450
  40.8 4.0 %collective-permute-start.7 = (f32[16,8,128]{2,1,0:T(8,128)S(1)}, f32[16,8,128]{2,1,0:T(8,128)S(1)}, u32[]{:S(2)}, u32[]{:S(2)}) collective-permute-start(f32[16,8,128]{2,1,0:T(8,128)S(1)} %get-tuple-element.32), channel_id=1, source_target_pairs={{0,12},{4,8},{8,4},{12,0},{1,13},{5,9},{9,5},{13,1},{2,14},{6,10},... | collective-permute-start | bytes 196616 | tf_op jit(solution)/shard_map/ppermute | solution.py:450

commit v3 on v2

--- a/solution.py
+++ b/solution.py
@@ -68,48 +68,75 @@
         )
 
 
+def column_forms(w0, w1, w2):
+    even, odd = w0 * (1 / 24) + w2 * (1 / 6), w1 * (1 / 12)
+    sides, middle = (w0 + w2) * (-1 / 6), w1 * (-1 / 6)
+    return w0 * 0.25, sides + middle, sides - middle, even + odd, even - odd, w2
+
+
+def column_points(fours):
+    d0, d1, d2, d3 = (fours[:-1, k] for k in range(4))
+    d4, d5 = fours[1:, 0], fours[1:, 1]
+    e1, e2 = d4 - 4 * d2, d3 - 4 * d1
+    e3, e4 = d4 - d2, 2 * (d3 - d1)
+    return 4 * (d0 - d2) + e3, e1 + e2, e1 - e2, e3 + e4, e3 - e4, (d5 - d3) - 2 * e4
+
+
+def column_outputs(m0, m1, m2, m3, m4, m5):
+    s1, t1, s3, t3 = m1 + m2, m1 - m2, m3 + m4, m3 - m4
+    return m0 + s1 + s3, t1 + 2 * t3, s1 + 4 * s3, t1 + 8 * t3 + m5
+
+
 def weights_kernel(states, *refs):
-    wi_out, wm_out, wo_out, wo_last, bias_out, sums_out = refs[6:12]
+    wi_out, wi_forms, wm_out, wo_out, bias_out, sums_out = refs[6:12]
     wi_ref, wm_ref, wo_ref, bi_ref, bm_ref, bo_ref = refs[12:18]
     arrive(fetch(refs[:6], refs[12:18], refs[18]))
     chans, hid = wi_ref.shape[2], wi_ref.shape[3]
-    terms = [split(jnp.concatenate([wi_ref[a, b] * 0.5 for b in range(3)], 1)) for a in range(3)]
-    high, low = [t[0] for t in terms], [t[1] for t in terms]
-    none = jnp.zeros_like(high[0])
-    upper = high + [none] + low + [none]
-    lower = high + [none] * 5
-    for r in range(NET):
+    taps = [[wi_ref[a, b] * 0.5 for b in range(3)] for a in range(3)]
+    wide_terms = [split(jnp.concatenate(taps[a], 1)) for a in range(3)]
+    form_terms = [[split(form) for form in column_forms(*taps[a])] for a in range(3)]
+    none = jnp.zeros((chans, 3 * hid), BF16)
+
+    def banded(pair, terms, empty, store):
         for g in range(PACK):
-            at = (g + r) % PACK * chans
-            wi_out[r, at : at + chans] = upper[g]
-            wi_out[r, hid + at : hid + at + chans] = lower[g]
+            rolled = (g - 2 * pair) % PACK >= 4
+            row = (g + PACK // 2) % PACK if rolled else g
+            for r in range(2):
+                a, low = row - 2 * pair - r, g - 2 * pair - r
+                store(r, g * chans, terms[a][int(rolled)] if 0 <= a < 3 else empty)
+                store(r, hid + g * chans, terms[low][0] if 0 <= low < 3 else empty)
+
+    for pair in range(NET // 2):
+
+        def store(r, at, value):
+            wi_out[pair, at : at + chans, r * 3 * hid : (r + 1) * 3 * hid] = value
+
+        banded(pair, wide_terms, none, store)
+        for point in range(6):
+
+            def store(r, at, value):
+                wi_forms[pair, point, at : at + chans, r * hid : (r + 1) * hid] = value
+
+            banded(pair, [t[point] for t in form_terms], none[:, :hid], store)
     for a in range(3):
-        w0, w1, w2 = (wm_ref[a, b].T * 0.5 for b in range(3))
-        even, odd = w0 * (1 / 24) + w2 * (1 / 6), w1 * (1 / 12)
-        sides = (w0 + w2) * (-1 / 6)
-        middle = w1 * (-1 / 6)
-        forms = (w0 * 0.25, sides + middle, sides - middle, even + odd, even - odd, w2)
+        forms = column_forms(*(wm_ref[a, b].T * 0.5 for b in range(3)))
         for point, form in enumerate(forms):
             both = jnp.concatenate(split(form), 1)
             wm_out[point, 2 * a * hid : (2 * a + 1) * hid] = both
             wm_out[point, (2 * a + 1) * hid : (2 * a + 2) * hid] = both
-    count = PACK + 2
     empty = jnp.zeros((chans, hid), F32)
-    for k in range(count):
-        for b in range(3):
-            band = jnp.concatenate(
-                [wo_ref[k - r, b] if 0 <= k - r < 3 else empty for r in range(PACK)], 0
-            ).T
-            high, low = split(band)
-            if b < 2:
-                lanes = slice(b * hid, (b + 1) * hid)
-                wo_out[2 * k * hid : (2 * k + 1) * hid, lanes] = high
-                wo_out[(2 * k + 1) * hid : (2 * k + 2) * hid, lanes] = high
-                wo_out[(2 * count + k) * hid : (2 * count + k + 1) * hid, lanes] = low
-            else:
-                both = jnp.concatenate([high, low], 1)
-                wo_last[2 * k * hid : (2 * k + 1) * hid] = both
-                wo_last[(2 * k + 1) * hid : (2 * k + 2) * hid] = both
+    group = lane_groups((hid, hid), 2 * chans)
+    for k in range(4):
+        pairs = [
+            [wo_ref[k - r, b] if 0 <= k - r < 3 else empty for r in range(2)] for b in range(3)
+        ]
+        one = jnp.concatenate(pairs[0] + pairs[1] + pairs[2] + pairs[0], 0).T
+        two = jnp.concatenate([empty] * 2 + pairs[1] + pairs[2] + [empty] * 2, 0).T
+        high = one.astype(BF16).astype(F32)
+        one = jnp.where(group < 3, high, one - high).astype(BF16)
+        both = jnp.concatenate([one, split(two)[1]], 1)
+        wo_out[2 * k * hid : (2 * k + 1) * hid] = both
+        wo_out[(2 * k + 1) * hid : (2 * k + 2) * hid] = both
     bias_out[0:1] = bi_ref[...].reshape(1, hid) * 0.5
     bias_out[1:2] = bm_ref[...].reshape(1, hid) * 0.5
     bias_out[2:3] = jnp.concatenate([bo_ref[...].reshape(1, chans)] * PACK, 1)
@@ -125,11 +152,11 @@
 def main_kernel(tm, *refs):
     mid_ref, even_ref, odd_ref = refs[:3]
     pars = refs[3 : 3 + tm]
-    bias_ref, wi_ref, wm_ref, wo_ref, wo_last, sums_ref = refs[3 + tm : 9 + tm]
+    bias_ref, wi_ref, wi_forms, wm_ref, wo_ref, sums_ref = refs[3 + tm : 9 + tm]
     outs = refs[9 + tm : 9 + 2 * tm]
     (
         rows_s, par_s, held_s, start_s, common_s, points_s, hid2_s, inputs_s, chunk_s,
-        in_bias, mid_bias, eps_s,
+        in_bias, mid_bias, eps_s, parts_s, turned_s, low_s,
     ) = refs[9 + 2 * tm :]
     rows, chans, depth = mid_ref.shape
     states, hid = par_s.shape[0], par_s.shape[1] // 2
@@ -178,23 +205,13 @@
     def packed_start(first):
         return rows_s[first : first + PACK].reshape(PACK * chans, depth).T
 
-    def first_conv(r, values):
-        group = lane_groups(values[0].shape, chans)
-        own = (group >= r) & (group <= r + 2)
-        left = []
-        for value in values:
-            turned = pltpu.roll(value, hid // 2, 1)
-            low = split(value)[1]
-            left.append(jnp.concatenate([jnp.where(own, value, turned).astype(BF16), low], 1))
-        return jnp.dot(jnp.concatenate(left, 0), wi_ref[r], preferred_element_type=F32)
+    def left_side(pair, value, turned, low):
+        group = lane_groups(value.shape, chans)
+        own = (group >= 2 * pair) & (group < 2 * pair + 4)
+        return jnp.concatenate([jnp.where(own, value, turned).astype(BF16), low], 1)
 
     def to_points(row, field):
-        fours = field.reshape(groups + 1, 4, states, hid)
-        d0, d1, d2, d3 = (fours[:groups, k] for k in range(4))
-        d4, d5 = fours[1:, 0], fours[1:, 1]
-        e1, e2 = d4 - 4 * d2, d3 - 4 * d1
-        e3, e4 = d4 - d2, 2 * (d3 - d1)
-        forms = (4 * (d0 - d2) + e3, e1 + e2, e1 - e2, e3 + e4, e3 - e4, (d5 - d3) - 2 * e4)
+        forms = column_points(field.reshape(groups + 1, 4, states, hid))
         for point, form in enumerate(forms):
             high, low = split(form.reshape(groups * states, hid))
             points_s[point, row, :, :hid] = high
@@ -214,11 +231,7 @@
                 )
                 both = jnp.dot(left, wm_ref[point], preferred_element_type=F32)
                 sums.append((both[:, :hid] + both[:, hid:]).reshape(step, groups, states, hid))
-            m0, m1, m2, m3, m4, m5 = sums
-            s1, t1, s3, t3 = m1 + m2, m1 - m2, m3 + m4, m3 - m4
-            field = jnp.stack(
-                [m0 + s1 + s3, t1 + 2 * t3, s1 + 4 * s3, t1 + 8 * t3 + m5], 2
-            ).reshape(step, wide, states, hid)
+            field = jnp.stack(column_outputs(*sums), 2).reshape(step, wide, states, hid)
             for r in range(step):
                 ok = in_field(row0 + row_first + first + r)
                 value = silu_of_double(field[r] + mid_bias[ok, col_first : col_first + wide])
@@ -230,17 +243,40 @@
         lax.fori_loop(0, count // step, body, 0)
 
     def noise(packs, width):
-        count = PACK + 2
-        both = [
-            jnp.concatenate([hid2_s[NET * p + k] for p in range(packs)], 0) for k in range(count)
+        units = PACK // 2 + (NET // 2) * (packs - 1)
+        left = jnp.concatenate(
+            [
+                jnp.concatenate([hid2_s[2 * u + k] for u in range(units)], 0)
+                for k in range(4)
+            ],
+            1,
+        )
+        taps = jnp.dot(left, wo_ref[...], preferred_element_type=F32)
+        taps = (taps[:, :hid] + taps[:, hid:]).reshape(units, wide, states, hid)
+        shape = (width, states, hid)
+        group = lane_groups(shape, 2 * chans)
+        one = [
+            jnp.where(
+                group == 1,
+                taps[u, 1 : width + 1],
+                jnp.where(group == 2, taps[u, 2 : width + 2], taps[u, :width]),
+            )
+            for u in range(units)
         ]
-        left = jnp.concatenate(both + [v[:, :hid] for v in both], 1)
-        two = jnp.dot(left, wo_ref[...], preferred_element_type=F32)
-        last = jnp.dot(left[:, : 2 * count * hid], wo_last[...], preferred_element_type=F32)
-        shape = (packs, wide, states, hid)
-        t0, t1 = two[:, :hid].reshape(shape), two[:, hid:].reshape(shape)
-        t2 = (last[:, :hid] + last[:, hid:]).reshape(shape)
-        return t0[:, :width] + t1[:, 1 : width + 1] + t2[:, 2 : width + 2] + out_bias
+
+        def turn(value, shift):
+            return pltpu.roll(value.reshape(width * states, hid), shift, 1).reshape(shape)
+
+        lower, even = group < 2, group % 2 == 0
+        values = []
+        for p in range(packs):
+            u0, u1, u2, u3 = one[NET // 2 * p : NET // 2 * p + 4]
+            v0 = jnp.where(lower, u0, u2) + turn(jnp.where(lower, u2, u0), hid // 2)
+            v1 = jnp.where(lower, u1, u3) + turn(jnp.where(lower, u3, u1), hid // 2)
+            other = jnp.where(even, v1, v0)
+            other = jnp.where(even, turn(other, hid - 2 * chans), turn(other, 2 * chans))
+            values.append(jnp.where(even, v0, v1) + other + out_bias)
+        return values
 
     state = lax.broadcasted_iota(jnp.int32, (1, states, hid), 1)
 
@@ -256,16 +292,22 @@
     for p in range(packs):
         start_s[p] = packed_start(NET * p)
 
-    def first_rows(r, _):
-        taps = first_conv(r, [start_s[p] for p in range(packs)])
+    near = wide + 8
+    for pair in range(NET // 2):
+        left = []
         for p in range(packs):
-            t0, t1, t2 = (
-                taps[p * depth : (p + 1) * depth, k * hid : (k + 1) * hid] for k in range(3)
-            )
-            common_s[NET * p + r] = t0 + pltpu.roll(t1, depth - 1, 0) + pltpu.roll(t2, depth - 2, 0)
-        return 0
-
-    lax.fori_loop(0, NET, first_rows, 0)
+            value = start_s[p, :near]
+            left.append(left_side(pair, value, pltpu.roll(value, hid // 2, 1), split(value)[1]))
+        taps = jnp.dot(jnp.concatenate(left, 0), wi_ref[pair], preferred_element_type=F32)
+        for p in range(packs):
+            for r in range(2):
+                t0, t1, t2 = (
+                    taps[p * near : (p + 1) * near, (3 * r + k) * hid : (3 * r + k + 1) * hid]
+                    for k in range(3)
+                )
+                common_s[NET * p + 2 * pair + r] = (
+                    t0 + pltpu.roll(t1, near - 1, 0) + pltpu.roll(t2, near - 2, 0)
+                )
 
     def first_points(i, _):
         ok = in_field(row0 - 5 + i)
@@ -288,23 +330,33 @@
         inputs_s[p, : reach_cols * states] = total
         inputs_s[p, reach_cols * states :] = jnp.zeros(((wide - reach_cols) * states, hid), F32)
 
-    def second_rows(r, _):
-        taps = first_conv(r, [inputs_s[p] for p in range(packs)])
-        width = cols + 4
+    fours = wide // 4 - 1
+    for point, form in enumerate(
+        zip(*(column_points(inputs_s[p].reshape(wide // 4, 4, states, hid)) for p in range(packs)))
+    ):
+        value = jnp.stack(form).reshape(packs * fours * states, hid)
+        parts_s[point] = value
+        turned_s[point] = pltpu.roll(value, hid // 2, 1)
+        low_s[point] = split(value)[1]
+
+    def second_rows(pair, _):
+        products = []
+        for point in range(6):
+            left = left_side(pair, parts_s[point], turned_s[point], low_s[point])
+            both = jnp.dot(left, wi_forms[pair, point], preferred_element_type=F32)
+            products.append(both.reshape(packs, fours, states, 2 * hid))
         for p in range(packs):
-            first = p * wide * states
-            t0, t1, t2 = (
-                taps[first + k * states : first + (k + width) * states, k * hid : (k + 1) * hid]
-                for k in range(3)
-            )
-            i = NET * p + r
-            ok = in_field(row0 - 2 + i)
-            value = (t0 + t1 + t2).reshape(width, states, hid) + in_bias[ok, 3 : 3 + width]
-            value = silu_of_double(value)
-            to_points(i, jnp.concatenate([value, jnp.zeros((8, states, hid), F32)], 0))
+            for r in range(2):
+                field = jnp.stack(
+                    column_outputs(*(m[p, :, :, r * hid : (r + 1) * hid] for m in products)), 1
+                ).reshape(4 * fours, states, hid)
+                i = NET * p + 2 * pair + r
+                ok = in_field(row0 - 2 + i)
+                value = silu_of_double(field + in_bias[ok, 3 : 3 + 4 * fours])
+                to_points(i, jnp.concatenate([value, jnp.zeros((8, states, hid), F32)], 0))
         return 0
 
-    lax.fori_loop(0, NET, second_rows, 0)
+    lax.fori_loop(0, NET // 2, second_rows, 0)
     second_hidden(rows + 2, 5, -1, 3)
 
     value = noise(1, cols)[0]
@@ -395,14 +447,13 @@
         lax.ppermute(par, "tm", [(i, i ^ k) for i in range(tm)]) for k in range(1, tm)
     ]
 
-    taps = (PACK + 2) * hid
     weights = kernel_call(
         functools.partial(weights_kernel, states),
         (
-            local((NET, 2 * hid, 3 * hid), BF16),
+            local((NET // 2, 2 * hid, 6 * hid), BF16),
+            local((NET // 2, 6, 2 * hid, 2 * hid), BF16),
             local((6, 6 * hid, 2 * hid), BF16),
-            local((3 * taps, 2 * hid), BF16),
-            local((2 * taps, 2 * hid), BF16),
+            local((8 * hid, 2 * hid), BF16),
             local((8, hid), F32),
             local((cols * states, cols * states), BF16),
         ),
@@ -419,11 +470,12 @@
         flops=10**7,
         read=8 * 10**6,
     )(*map(in_hbm, (w_in.transpose(0, 1, 3, 2), w_mid, w_out, b_in, b_mid, b_out)))
-    wi, wm, wo, wo_last, bias, sums = weights
+    wi, wi_forms, wm, wo, bias, sums = weights
 
     groups = (cols + 8) // 4
     wide = 4 * groups
     width = here * cols
+    parts = (rows + HALO - 2) // NET * (groups - 1) * states
     chunks = kernel_call(
         functools.partial(main_kernel, tm),
         tuple(local((chans, rows, width), F32) for _ in range(tm)),
@@ -433,7 +485,7 @@
             pltpu.VMEM((states, 2 * hid), F32),
             pltpu.VMEM((tm, here, 2 * hid), F32),
             pltpu.VMEM(((rows + 2 * HALO - 2) // NET, depth, hid), F32),
-            pltpu.VMEM((rows + 10, depth, hid), F32),
+            pltpu.VMEM((rows + 10, wide + 8, hid), F32),
             pltpu.VMEM((6, rows + 10, groups * states, 2 * hid), BF16),
             pltpu.VMEM((rows + 8, wide * states, 2 * hid), BF16),
             pltpu.VMEM(((rows + HALO - 2) // NET, wide * states, hid), F32),
@@ -441,10 +493,11 @@
             pltpu.VMEM((2, wide + 4, states, hid), F32),
             pltpu.VMEM((2, wide + 3, states, hid), F32),
             pltpu.VMEM((cols + HALO, states, hid), F32),
+            *(pltpu.VMEM((6, parts, hid), kind) for kind in (F32, F32, BF16)),
         ),
         flops=10**10,
         read=8 * 10**6,
-    )(mid, even, odd, *pars, bias, wi, wm, wo, wo_last, sums)
+    )(mid, even, odd, *pars, bias, wi, wi_forms, wm, wo, sums)
 
     blocks = [chunks[0]] + [
         lax.ppermute(chunks[k], "tm", [(i, i ^ k) for i in range(tm)]) for k in range(1, tm)

time: 45.9 us -> 42 us (0.915)
  Pallas kernels: 32.6 us -> 28.7 us
    pallas_call x1, Pallas kernels: 28.4 us -> 24.6 us  [on_device(): kernel_call(functools.partial(main_kernel, tm), tuple((local((chans, rows...]
where the time goes in v3:
time: 42 us; the launch traced here: 41.8 us
  Pallas kernels  28.7 us (68%)
  starting transfers between devices  9.62 us (23%)
  waiting for transfers between devices  3.44 us (8%)
    pallas_call x1, Pallas kernels, on_device(): kernel_call(functools.partial(main_kernel, tm), tuple((local((chans, rows...  24.6 us
    ppermute x1, starting transfers between devices, on_device(): odd = lax.ppermute(odd, 'space', pairs + [(b, a) for a, b in pairs])  4.48 us
    ppermute x3, waiting for transfers between devices, on_device(): lax.ppermute(chunks[k], 'tm', [(i, i ^ k) for i in range(tm)])  3.42 us
    ppermute x3, starting transfers between devices, on_device(): lax.ppermute(par, 'tm', [(i, i ^ k) for i in range(tm)])  2.87 us
    ppermute x3, starting transfers between devices, on_device(): lax.ppermute(chunks[k], 'tm', [(i, i ^ k) for i in range(tm)])  2.21 us
    pallas_call x1, Pallas kernels, on_device(): kernel_call(functools.partial(weights_kernel, states), (local((NET // 2,...  2.1 us
    pallas_call x1, Pallas kernels, on_device(): kernel_call(pack_kernel, (local((rows, chans, depth), F32), edge, edge, l...  1.12 us
    pallas_call x1, Pallas kernels, on_device(): kernel_call(functools.partial(join_kernel, tm), shape((here, chans, rows,...  0.86 us
  transfers between devices with their start and end apart: 8, of which 2 were waited for; matrix products, arithmetic and copies ran while one was open for 0% of the time, Pallas kernels for 5%

profile of v3, /device:TPU:9, one launch (start us, length us, event | category | flops | bytes accessed | tf_op | source)
XLA Modules:
  0.0 41.8 jit_solution(13687050583424700441)
XLA Ops:
  0.0 1.1 %shard_map.100 = (f32[8,16,128]{2,1,0:T(8,128)S(1)}, f32[6,16,128]{2,1,0:T(8,128)S(1)}, f32[6,16,128]{2,1,0:T(8,128)S(1)}, f32[2,256]{1,0:T(2,128)S(1)}) custom-call(f32[16,8,256]{2,1,0:T(8,128)} %refs_0_.1, f32[2,128]{1,0:T(2,128)} %refs_1_.2, f32[2]{0:T(128)} %refs_2_.2, f32[2]{0:T(128)} %refs_3_.2), custom_call_target="tpu_custom_call" | custom-call | bytes 1000000 | tf_op jit(solution)/shard_map/pallas_call | solution.py:430
  1.1 0.1 collective-permute-start
  1.2 4.5 %collective-permute-start.1 = (f32[6,16,128]{2,1,0:T(8,128)S(1)}, f32[6,16,128]{2,1,0:T(8,128)S(1)}, u32[]{:S(2)}, u32[]{:S(2)}) collective-permute-start(f32[6,16,128]{2,1,0:T(8,128)S(1)} %get-tuple-element.21), channel_id=1, source_target_pairs={{1,2},{2,1},{5,6},{6,5},{9,10},{10,9},{13,14},{14,13},{17,18},{18,... | collective-permute-start | bytes 147464 | tf_op jit(solution)/shard_map/ppermute | solution.py:445
  5.7 2.4 %collective-permute-start.4 = (f32[2,256]{1,0:T(2,128)S(1)}, f32[2,256]{1,0:T(2,128)S(1)}, u32[]{:S(2)}, u32[]{:S(2)}) collective-permute-start(f32[2,256]{1,0:T(2,128)S(1)} %get-tuple-element.22.refs_3_), channel_id=1, source_target_pairs={{0,12},{4,8},{8,4},{12,0},{1,13},{5,9},{9,5},{13,1},{2,14},{6,10},... | collective-permute-start | bytes 6152 | tf_op jit(solution)/shard_map/ppermute | solution.py:447
  8.1 0.3 collective-permute-start.3
  8.3 0.2 collective-permute-start.2
  8.6 2.1 %shard_map.101 = (bf16[3,256,768]{2,1,0:T(8,128)(2,1)S(1)}, bf16[3,6,256,256]{3,2,1,0:T(8,128)(2,1)S(1)}, bf16[6,768,256]{2,1,0:T(8,128)(2,1)S(1)}, bf16[1024,25...) custom-call(f32[3,3,16,128]{3,2,1,0:T(8,128)} %bitcast.1, f32[3,3,128,128]{3,2,1,0:T(8,128)} %refs_1_.3, ...), custom_call_target="tpu_custom_call" | custom-call | flops 10000000 | bytes 8000000 | tf_op jit(solution)/shard_map/pallas_call | solution.py:450
  10.7 0.0 collective-permute-done.4.refs_6_
  10.7 0.0 collective-permute-done.3.refs_5_
  10.7 0.0 collective-permute-done.2.refs_4_
  10.7 0.0 collective-permute-done.refs_1_
  10.7 0.0 collective-permute-done.1.refs_2_
  10.7 24.6 %shard_map.102 = (f32[16,8,128]{2,1,0:T(8,128)S(1)}, f32[16,8,128]{2,1,0:T(8,128)S(1)}, f32[16,8,128]{2,1,0:T(8,128)S(1)}, f32[16,8,128]{2,1,0:T(8,128)S(1)}) custom-call(f32[8,16,128]{2,1,0:T(8,128)S(1)} %get-tuple-element.19.refs_0_, f32[6,16,128]{2,1,0:T(8,128)S(1)} %collective-permute-done.refs_1_, f32[6,16,128]{2,1,0:T(8,128)S(1)} %collective-permute-done.1.refs_2_, ...), custom_call_target="tpu_custom_call" | custom-call | flops 10000000000 | bytes 8000000 | tf_op jit(solution)/shard_map/pallas_call | solution.py:479
  35.3 0.4 collective-permute-start.5
  35.7 1.2 %collective-permute-start.6 = (f32[16,8,128]{2,1,0:T(8,128)S(1)}, f32[16,8,128]{2,1,0:T(8,128)S(1)}, u32[]{:S(2)}, u32[]{:S(2)}) collective-permute-start(f32[16,8,128]{2,1,0:T(8,128)S(1)} %get-tuple-element.31), channel_id=1, source_target_pairs={{0,8},{4,12},{8,0},{12,4},{1,9},{5,13},{9,1},{13,5},{2,10},{6,14},... | collective-permute-start | bytes 196616 | tf_op jit(solution)/shard_map/ppermute | solution.py:503
  36.9 0.6 %collective-permute-start.7 = (f32[16,8,128]{2,1,0:T(8,128)S(1)}, f32[16,8,128]{2,1,0:T(8,128)S(1)}, u32[]{:S(2)}, u32[]{:S(2)}) collective-permute-start(f32[16,8,128]{2,1,0:T(8,128)S(1)} %get-tuple-element.32), channel_id=1, source_target_pairs={{0,12},{4,8},{8,4},{12,0},{1,13},{5,9},{9,5},{13,1},{2,14},{6,10},... | collective-permute-start | bytes 196616 | tf_op jit(solution)/shard_map/ppermute | solution.py:503
  37.5 0.0 collective-permute-done.5.refs_1_
  37.5 1.6 %collective-permute-done.6.refs_2_ = f32[16,8,128]{2,1,0:T(8,128)S(1)} collective-permute-done((f32[16,8,128]{2,1,0:T(8,128)S(1)}, f32[16,8,128]{2,1,0:T(8,128)S(1)}, u32[]{:S(2)}, u32[]{:S(2)}) %collective-permute-start.6) | collective-permute-done | bytes 65568 | tf_op jit(solution)/shard_map/ppermute | solution.py:503
  39.2 1.8 %collective-permute-done.7.refs_3_ = f32[16,8,128]{2,1,0:T(8,128)S(1)} collective-permute-done((f32[16,8,128]{2,1,0:T(8,128)S(1)}, f32[16,8,128]{2,1,0:T(8,128)S(1)}, u32[]{:S(2)}, u32[]{:S(2)}) %collective-permute-start.7) | collective-permute-done | bytes 65568 | tf_op jit(solution)/shard_map/ppermute | solution.py:503
  41.0 0.9 %shard_map.103 = f32[2,16,8,256]{3,2,1,0:T(8,128)} custom-call(f32[16,8,128]{2,1,0:T(8,128)S(1)} %get-tuple-element.29.refs_0_, f32[16,8,128]{2,1,0:T(8,128)S(1)} %collective-permute-done.5.refs_1_, f32[16,8,128]{2,1,0:T(8,128)S(1)} %collective-permute-done.6.refs_2_, f32[16,8,128]{2,1,0:T(8,128)S(1)} %collective-permute-done.7.refs_3_), custom_call_target="tpu_custom_call" | custom-call | bytes 1000000 | tf_op jit(solution)/shard_map/pallas_call | solution.py:505
Async XLA Ops:
  1.1 9.6 %collective-permute-start = (f32[6,16,128]{2,1,0:T(8,128)S(1)}, f32[6,16,128]{2,1,0:T(8,128)S(1)}, u32[]{:S(2)}, u32[]{:S(2)}) collective-permute-start(f32[6,16,128]{2,1,0:T(8,128)S(1)} %get-tuple-element.20), channel_id=1, source_target_pairs={{0,1},{1,0},{2,3},{3,2},{4,5},{5,4},{6,7},{7,6},{8,9},{9,8},{10,11... | collective-permute-start | bytes 147464 | tf_op jit(solution)/shard_map/ppermute | solution.py:443
  1.2 9.5 %collective-permute-start.1 = (f32[6,16,128]{2,1,0:T(8,128)S(1)}, f32[6,16,128]{2,1,0:T(8,128)S(1)}, u32[]{:S(2)}, u32[]{:S(2)}) collective-permute-start(f32[6,16,128]{2,1,0:T(8,128)S(1)} %get-tuple-element.21), channel_id=1, source_target_pairs={{1,2},{2,1},{5,6},{6,5},{9,10},{10,9},{13,14},{14,13},{17,18},{18,... | collective-permute-start | bytes 147464 | tf_op jit(solution)/shard_map/ppermute | solution.py:445
  5.7 5.0 %collective-permute-start.4 = (f32[2,256]{1,0:T(2,128)S(1)}, f32[2,256]{1,0:T(2,128)S(1)}, u32[]{:S(2)}, u32[]{:S(2)}) collective-permute-start(f32[2,256]{1,0:T(2,128)S(1)} %get-tuple-element.22.refs_3_), channel_id=1, source_target_pairs={{0,12},{4,8},{8,4},{12,0},{1,13},{5,9},{9,5},{13,1},{2,14},{6,10},... | collective-permute-start | bytes 6152 | tf_op jit(solution)/shard_map/ppermute | solution.py:447
  8.1 2.6 %collective-permute-start.3 = (f32[2,256]{1,0:T(2,128)S(1)}, f32[2,256]{1,0:T(2,128)S(1)}, u32[]{:S(2)}, u32[]{:S(2)}) collective-permute-start(f32[2,256]{1,0:T(2,128)S(1)} %get-tuple-element.22.refs_3_), channel_id=1, source_target_pairs={{0,8},{4,12},{8,0},{12,4},{1,9},{5,13},{9,1},{13,5},{2,10},{6,14},... | collective-permute-start | bytes 6152 | tf_op jit(solution)/shard_map/ppermute | solution.py:447
  8.3 2.4 %collective-permute-start.2 = (f32[2,256]{1,0:T(2,128)S(1)}, f32[2,256]{1,0:T(2,128)S(1)}, u32[]{:S(2)}, u32[]{:S(2)}) collective-permute-start(f32[2,256]{1,0:T(2,128)S(1)} %get-tuple-element.22.refs_3_), channel_id=1, source_target_pairs={{0,4},{4,0},{8,12},{12,8},{1,5},{5,1},{9,13},{13,9},{2,6},{6,2},{1... | collective-permute-start | bytes 6152 | tf_op jit(solution)/shard_map/ppermute | solution.py:447
  35.3 2.2 %collective-permute-start.5 = (f32[16,8,128]{2,1,0:T(8,128)S(1)}, f32[16,8,128]{2,1,0:T(8,128)S(1)}, u32[]{:S(2)}, u32[]{:S(2)}) collective-permute-start(f32[16,8,128]{2,1,0:T(8,128)S(1)} %get-tuple-element.30), channel_id=1, source_target_pairs={{0,4},{4,0},{8,12},{12,8},{1,5},{5,1},{9,13},{13,9},{2,6},{6,2},{1... | collective-permute-start | bytes 196616 | tf_op jit(solution)/shard_map/ppermute | solution.py:503
  35.7 3.5 %collective-permute-start.6 = (f32[16,8,128]{2,1,0:T(8,128)S(1)}, f32[16,8,128]{2,1,0:T(8,128)S(1)}, u32[]{:S(2)}, u32[]{:S(2)}) collective-permute-start(f32[16,8,128]{2,1,0:T(8,128)S(1)} %get-tuple-element.31), channel_id=1, source_target_pairs={{0,8},{4,12},{8,0},{12,4},{1,9},{5,13},{9,1},{13,5},{2,10},{6,14},... | collective-permute-start | bytes 196616 | tf_op jit(solution)/shard_map/ppermute | solution.py:503
  36.9 4.0 %collective-permute-start.7 = (f32[16,8,128]{2,1,0:T(8,128)S(1)}, f32[16,8,128]{2,1,0:T(8,128)S(1)}, u32[]{:S(2)}, u32[]{:S(2)}) collective-permute-start(f32[16,8,128]{2,1,0:T(8,128)S(1)} %get-tuple-element.32), channel_id=1, source_target_pairs={{0,12},{4,8},{8,4},{12,0},{1,13},{5,9},{9,5},{13,1},{2,14},{6,10},... | collective-permute-start | bytes 196616 | tf_op jit(solution)/shard_map/ppermute | solution.py:503

commit v4 on v3

--- a/solution.py
+++ b/solution.py
@@ -9,6 +9,7 @@
 REACH = 3
 HALO = 2 * REACH
 PACK = 8
+PIECE = 2
 NET = PACK - 2
 OFF = -1e30
 VMEM_LIMIT = 44 * 2**20
@@ -74,9 +75,9 @@
     return w0 * 0.25, sides + middle, sides - middle, even + odd, even - odd, w2
 
 
-def column_points(fours):
-    d0, d1, d2, d3 = (fours[:-1, k] for k in range(4))
-    d4, d5 = fours[1:, 0], fours[1:, 1]
+def column_points(fours, behind):
+    d0, d1, d2, d3 = (fours[:, k] for k in range(4))
+    d4, d5 = (jnp.concatenate([fours[1:, k], behind[:1, k]], 0) for k in range(2))
     e1, e2 = d4 - 4 * d2, d3 - 4 * d1
     e3, e4 = d4 - d2, 2 * (d3 - d1)
     return 4 * (d0 - d2) + e3, e1 + e2, e1 - e2, e3 + e4, e3 - e4, (d5 - d3) - 2 * e4
@@ -210,37 +211,46 @@
         own = (group >= 2 * pair) & (group < 2 * pair + 4)
         return jnp.concatenate([jnp.where(own, value, turned).astype(BF16), low], 1)
 
-    def to_points(row, field):
-        forms = column_points(field.reshape(groups + 1, 4, states, hid))
-        for point, form in enumerate(forms):
-            high, low = split(form.reshape(groups * states, hid))
-            points_s[point, row, :, :hid] = high
-            points_s[point, row, :, hid:] = low
-
-    def second_hidden(count, step, row_first, col_first):
-        def body(c, _):
-            first = c * step
-            sums = []
-            for point in range(6):
-                left = jnp.concatenate(
-                    [
-                        points_s[point, pl.ds(first + a, step)].reshape(step * groups * states, 2 * hid)
-                        for a in range(3)
-                    ],
-                    1,
-                )
-                both = jnp.dot(left, wm_ref[point], preferred_element_type=F32)
-                sums.append((both[:, :hid] + both[:, hid:]).reshape(step, groups, states, hid))
-            field = jnp.stack(column_outputs(*sums), 2).reshape(step, wide, states, hid)
-            for r in range(step):
-                ok = in_field(row0 + row_first + first + r)
-                value = silu_of_double(field[r] + mid_bias[ok, col_first : col_first + wide])
-                high, low = split(value.reshape(wide * states, hid))
-                hid2_s[first + r, :, :hid] = high
-                hid2_s[first + r, :, hid:] = low
-            return 0
-
-        lax.fori_loop(0, count // step, body, 0)
+    def pieces(count):
+        return [(first, min(first + PIECE, count)) for first in range(0, count, PIECE)]
+
+    def to_points(row, field, behind):
+        for first, last in reversed(pieces(groups)):
+            fours = field(first, last)
+            for point, form in enumerate(column_points(fours, behind)):
+                high, low = split(form.reshape((last - first) * states, hid))
+                points_s[point, row, first * states : last * states, :hid] = high
+                points_s[point, row, first * states : last * states, hid:] = low
+            behind = fours
+
+    def second_hidden(chosen, row_first, col_first, beside=()):
+        beside = list(beside)
+        step = len(chosen)
+        sums = []
+        for point in range(6):
+            left = jnp.concatenate(
+                [
+                    jnp.concatenate([points_s[point, i + a] for i in chosen], 0)
+                    for a in range(3)
+                ],
+                1,
+            )
+            both = jnp.dot(left, wm_ref[point], preferred_element_type=F32)
+            sums.append(both.reshape(step, groups, states, 2 * hid))
+            if beside:
+                beside.pop(0)()
+        for r, i in enumerate(chosen):
+            ok = in_field(row0 + row_first + i)
+            for first, last in pieces(groups):
+                parts = [m[r, first:last] for m in sums]
+                parts = [m[:, :, :hid] + m[:, :, hid:] for m in parts]
+                size = 4 * (last - first)
+                field = jnp.stack(column_outputs(*parts), 1).reshape(size, states, hid)
+                bias = mid_bias[ok, col_first + 4 * first : col_first + 4 * last]
+                high, low = split(silu_of_double(field + bias).reshape(size * states, hid))
+                place = slice(4 * first * states, 4 * last * states)
+                hid2_s[i, place, :hid] = high
+                hid2_s[i, place, hid:] = low
 
     def noise(packs, width):
         units = PACK // 2 + (NET // 2) * (packs - 1)
@@ -309,13 +319,23 @@
                     t0 + pltpu.roll(t1, near - 1, 0) + pltpu.roll(t2, near - 2, 0)
                 )
 
-    def first_points(i, _):
+    def first_points(i):
         ok = in_field(row0 - 5 + i)
-        to_points(i, silu_of_double(common_s[i, : wide + 4][:, None, :] + in_bias[ok]))
-        return 0
-
-    lax.fori_loop(0, rows + 10, first_points, 0)
-    second_hidden(rows + 8, 4, -4, 0)
+
+        def field(first, last):
+            place = slice(4 * first, 4 * last)
+            value = silu_of_double(common_s[i, place][:, None, :] + in_bias[ok, place])
+            return value.reshape(last - first, 4, states, hid)
+
+        to_points(i, field, field(groups, groups + 1))
+
+    step = 4
+    calls = [functools.partial(first_points, i) for i in range(rows + 10)]
+    for call in calls[: step + 2]:
+        call()
+    for first in range(0, rows + 8, step):
+        ahead = first + step + 2
+        second_hidden(range(first, first + step), -4, 0, calls[ahead : ahead + step])
 
     packs = inputs_s.shape[0]
     value = noise(packs, reach_cols)
@@ -331,15 +351,15 @@
         inputs_s[p, reach_cols * states :] = jnp.zeros(((wide - reach_cols) * states, hid), F32)
 
     fours = wide // 4 - 1
-    for point, form in enumerate(
-        zip(*(column_points(inputs_s[p].reshape(wide // 4, 4, states, hid)) for p in range(packs)))
-    ):
+    packed = [inputs_s[p].reshape(groups, 4, states, hid) for p in range(packs)]
+    packed = [column_points(v[:fours], v[fours:]) for v in packed]
+    for point, form in enumerate(zip(*packed)):
         value = jnp.stack(form).reshape(packs * fours * states, hid)
         parts_s[point] = value
         turned_s[point] = pltpu.roll(value, hid // 2, 1)
         low_s[point] = split(value)[1]
 
-    def second_rows(pair, _):
+    def second_rows(pair):
         products = []
         for point in range(6):
             left = left_side(pair, parts_s[point], turned_s[point], low_s[point])
@@ -347,17 +367,25 @@
             products.append(both.reshape(packs, fours, states, 2 * hid))
         for p in range(packs):
             for r in range(2):
-                field = jnp.stack(
-                    column_outputs(*(m[p, :, :, r * hid : (r + 1) * hid] for m in products)), 1
-                ).reshape(4 * fours, states, hid)
                 i = NET * p + 2 * pair + r
                 ok = in_field(row0 - 2 + i)
-                value = silu_of_double(field + in_bias[ok, 3 : 3 + 4 * fours])
-                to_points(i, jnp.concatenate([value, jnp.zeros((8, states, hid), F32)], 0))
-        return 0
-
-    lax.fori_loop(0, NET // 2, second_rows, 0)
-    second_hidden(rows + 2, 5, -1, 3)
+
+                def field(first, last, p=p, r=r, ok=ok):
+                    last = min(last, fours)
+                    parts = [m[p, first:last, :, r * hid : (r + 1) * hid] for m in products]
+                    value = jnp.stack(column_outputs(*parts), 1)
+                    bias = in_bias[ok, 3 + 4 * first : 3 + 4 * last].reshape(value.shape)
+                    value = silu_of_double(value + bias)
+                    return jnp.concatenate([value, none], 0) if last == fours else value
+
+                none = jnp.zeros((1, 4, states, hid), F32)
+                to_points(i, field, none)
+
+    calls = [functools.partial(second_rows, pair) for pair in range(NET // 2)]
+    calls[0]()
+    calls[1]()
+    second_hidden([0, 1, NET, NET + 1], -1, 3, calls[2:])
+    second_hidden([2, 3, 4, 5, NET + 2, NET + 3], -1, 3)
 
     value = noise(1, cols)[0]
     size = cols * states

time: 42 us -> 39.3 us (0.936)
  Pallas kernels: 28.7 us -> 26 us
    pallas_call x1, Pallas kernels: 24.6 us -> 22 us  [on_device(): kernel_call(functools.partial(main_kernel, tm), tuple((local((chans, rows...]
where the time goes in v4:
time: 39.3 us; the launch traced here: 39.2 us
  Pallas kernels  26 us (66%)
  starting transfers between devices  9.62 us (24%)
  waiting for transfers between devices  3.43 us (9%)
    pallas_call x1, Pallas kernels, on_device(): kernel_call(functools.partial(main_kernel, tm), tuple((local((chans, rows...  22 us
    ppermute x1, starting transfers between devices, on_device(): odd = lax.ppermute(odd, 'space', pairs + [(b, a) for a, b in pairs])  4.48 us
    ppermute x3, waiting for transfers between devices, on_device(): lax.ppermute(chunks[k], 'tm', [(i, i ^ k) for i in range(tm)])  3.42 us
    ppermute x3, starting transfers between devices, on_device(): lax.ppermute(par, 'tm', [(i, i ^ k) for i in range(tm)])  2.87 us
    ppermute x3, starting transfers between devices, on_device(): lax.ppermute(chunks[k], 'tm', [(i, i ^ k) for i in range(tm)])  2.21 us
    pallas_call x1, Pallas kernels, on_device(): kernel_call(functools.partial(weights_kernel, states), (local((NET // 2,...  2.1 us
    pallas_call x1, Pallas kernels, on_device(): kernel_call(pack_kernel, (local((rows, chans, depth), F32), edge, edge, l...  1.12 us
    pallas_call x1, Pallas kernels, on_device(): kernel_call(functools.partial(join_kernel, tm), shape((here, chans, rows,...  0.86 us
  transfers between devices with their start and end apart: 8, of which 2 were waited for; matrix products, arithmetic and copies ran while one was open for 0% of the time, Pallas kernels for 5%

profile of v4, /device:TPU:9, one launch (start us, length us, event | category | flops | bytes accessed | tf_op | source)
XLA Modules:
  0.0 39.2 jit_solution(1844863375861566950)
XLA Ops:
  0.0 1.1 %shard_map.100 = (f32[8,16,128]{2,1,0:T(8,128)S(1)}, f32[6,16,128]{2,1,0:T(8,128)S(1)}, f32[6,16,128]{2,1,0:T(8,128)S(1)}, f32[2,256]{1,0:T(2,128)S(1)}) custom-call(f32[16,8,256]{2,1,0:T(8,128)} %refs_0_.1, f32[2,128]{1,0:T(2,128)} %refs_1_.2, f32[2]{0:T(128)} %refs_2_.2, f32[2]{0:T(128)} %refs_3_.2), custom_call_target="tpu_custom_call" | custom-call | bytes 1000000 | tf_op jit(solution)/shard_map/pallas_call | solution.py:458
  1.1 0.1 collective-permute-start
  1.2 4.5 %collective-permute-start.1 = (f32[6,16,128]{2,1,0:T(8,128)S(1)}, f32[6,16,128]{2,1,0:T(8,128)S(1)}, u32[]{:S(2)}, u32[]{:S(2)}) collective-permute-start(f32[6,16,128]{2,1,0:T(8,128)S(1)} %get-tuple-element.21), channel_id=1, source_target_pairs={{1,2},{2,1},{5,6},{6,5},{9,10},{10,9},{13,14},{14,13},{17,18},{18,... | collective-permute-start | bytes 147464 | tf_op jit(solution)/shard_map/ppermute | solution.py:473
  5.7 2.4 %collective-permute-start.4 = (f32[2,256]{1,0:T(2,128)S(1)}, f32[2,256]{1,0:T(2,128)S(1)}, u32[]{:S(2)}, u32[]{:S(2)}) collective-permute-start(f32[2,256]{1,0:T(2,128)S(1)} %get-tuple-element.22.refs_3_), channel_id=1, source_target_pairs={{0,12},{4,8},{8,4},{12,0},{1,13},{5,9},{9,5},{13,1},{2,14},{6,10},... | collective-permute-start | bytes 6152 | tf_op jit(solution)/shard_map/ppermute | solution.py:475
  8.1 0.3 collective-permute-start.3
  8.3 0.2 collective-permute-start.2
  8.6 2.1 %shard_map.101 = (bf16[3,256,768]{2,1,0:T(8,128)(2,1)S(1)}, bf16[3,6,256,256]{3,2,1,0:T(8,128)(2,1)S(1)}, bf16[6,768,256]{2,1,0:T(8,128)(2,1)S(1)}, bf16[1024,25...) custom-call(f32[3,3,16,128]{3,2,1,0:T(8,128)} %bitcast.1, f32[3,3,128,128]{3,2,1,0:T(8,128)} %refs_1_.3, ...), custom_call_target="tpu_custom_call" | custom-call | flops 10000000 | bytes 8000000 | tf_op jit(solution)/shard_map/pallas_call | solution.py:478
  10.7 0.0 collective-permute-done.4.refs_6_
  10.7 0.0 collective-permute-done.3.refs_5_
  10.7 0.0 collective-permute-done.2.refs_4_
  10.7 0.0 collective-permute-done.refs_1_
  10.7 0.0 collective-permute-done.1.refs_2_
  10.7 22.0 %shard_map.102 = (f32[16,8,128]{2,1,0:T(8,128)S(1)}, f32[16,8,128]{2,1,0:T(8,128)S(1)}, f32[16,8,128]{2,1,0:T(8,128)S(1)}, f32[16,8,128]{2,1,0:T(8,128)S(1)}) custom-call(f32[8,16,128]{2,1,0:T(8,128)S(1)} %get-tuple-element.19.refs_0_, f32[6,16,128]{2,1,0:T(8,128)S(1)} %collective-permute-done.refs_1_, f32[6,16,128]{2,1,0:T(8,128)S(1)} %collective-permute-done.1.refs_2_, ...), custom_call_target="tpu_custom_call" | custom-call | flops 10000000000 | bytes 8000000 | tf_op jit(solution)/shard_map/pallas_call | solution.py:507
  32.7 0.4 collective-permute-start.5
  33.0 1.2 %collective-permute-start.6 = (f32[16,8,128]{2,1,0:T(8,128)S(1)}, f32[16,8,128]{2,1,0:T(8,128)S(1)}, u32[]{:S(2)}, u32[]{:S(2)}) collective-permute-start(f32[16,8,128]{2,1,0:T(8,128)S(1)} %get-tuple-element.31), channel_id=1, source_target_pairs={{0,8},{4,12},{8,0},{12,4},{1,9},{5,13},{9,1},{13,5},{2,10},{6,14},... | collective-permute-start | bytes 196616 | tf_op jit(solution)/shard_map/ppermute | solution.py:531
  34.3 0.6 %collective-permute-start.7 = (f32[16,8,128]{2,1,0:T(8,128)S(1)}, f32[16,8,128]{2,1,0:T(8,128)S(1)}, u32[]{:S(2)}, u32[]{:S(2)}) collective-permute-start(f32[16,8,128]{2,1,0:T(8,128)S(1)} %get-tuple-element.32), channel_id=1, source_target_pairs={{0,12},{4,8},{8,4},{12,0},{1,13},{5,9},{9,5},{13,1},{2,14},{6,10},... | collective-permute-start | bytes 196616 | tf_op jit(solution)/shard_map/ppermute | solution.py:531
  34.9 0.0 collective-permute-done.5.refs_1_
  34.9 1.6 %collective-permute-done.6.refs_2_ = f32[16,8,128]{2,1,0:T(8,128)S(1)} collective-permute-done((f32[16,8,128]{2,1,0:T(8,128)S(1)}, f32[16,8,128]{2,1,0:T(8,128)S(1)}, u32[]{:S(2)}, u32[]{:S(2)}) %collective-permute-start.6) | collective-permute-done | bytes 65568 | tf_op jit(solution)/shard_map/ppermute | solution.py:531
  36.5 1.8 %collective-permute-done.7.refs_3_ = f32[16,8,128]{2,1,0:T(8,128)S(1)} collective-permute-done((f32[16,8,128]{2,1,0:T(8,128)S(1)}, f32[16,8,128]{2,1,0:T(8,128)S(1)}, u32[]{:S(2)}, u32[]{:S(2)}) %collective-permute-start.7) | collective-permute-done | bytes 65568 | tf_op jit(solution)/shard_map/ppermute | solution.py:531
  38.3 0.9 %shard_map.103 = f32[2,16,8,256]{3,2,1,0:T(8,128)} custom-call(f32[16,8,128]{2,1,0:T(8,128)S(1)} %get-tuple-element.29.refs_0_, f32[16,8,128]{2,1,0:T(8,128)S(1)} %collective-permute-done.5.refs_1_, f32[16,8,128]{2,1,0:T(8,128)S(1)} %collective-permute-done.6.refs_2_, f32[16,8,128]{2,1,0:T(8,128)S(1)} %collective-permute-done.7.refs_3_), custom_call_target="tpu_custom_call" | custom-call | bytes 1000000 | tf_op jit(solution)/shard_map/pallas_call | solution.py:533
Async XLA Ops:
  1.1 9.6 %collective-permute-start = (f32[6,16,128]{2,1,0:T(8,128)S(1)}, f32[6,16,128]{2,1,0:T(8,128)S(1)}, u32[]{:S(2)}, u32[]{:S(2)}) collective-permute-start(f32[6,16,128]{2,1,0:T(8,128)S(1)} %get-tuple-element.20), channel_id=1, source_target_pairs={{0,1},{1,0},{2,3},{3,2},{4,5},{5,4},{6,7},{7,6},{8,9},{9,8},{10,11... | collective-permute-start | bytes 147464 | tf_op jit(solution)/shard_map/ppermute | solution.py:471
  1.2 9.5 %collective-permute-start.1 = (f32[6,16,128]{2,1,0:T(8,128)S(1)}, f32[6,16,128]{2,1,0:T(8,128)S(1)}, u32[]{:S(2)}, u32[]{:S(2)}) collective-permute-start(f32[6,16,128]{2,1,0:T(8,128)S(1)} %get-tuple-element.21), channel_id=1, source_target_pairs={{1,2},{2,1},{5,6},{6,5},{9,10},{10,9},{13,14},{14,13},{17,18},{18,... | collective-permute-start | bytes 147464 | tf_op jit(solution)/shard_map/ppermute | solution.py:473
  5.7 5.0 %collective-permute-start.4 = (f32[2,256]{1,0:T(2,128)S(1)}, f32[2,256]{1,0:T(2,128)S(1)}, u32[]{:S(2)}, u32[]{:S(2)}) collective-permute-start(f32[2,256]{1,0:T(2,128)S(1)} %get-tuple-element.22.refs_3_), channel_id=1, source_target_pairs={{0,12},{4,8},{8,4},{12,0},{1,13},{5,9},{9,5},{13,1},{2,14},{6,10},... | collective-permute-start | bytes 6152 | tf_op jit(solution)/shard_map/ppermute | solution.py:475
  8.1 2.6 %collective-permute-start.3 = (f32[2,256]{1,0:T(2,128)S(1)}, f32[2,256]{1,0:T(2,128)S(1)}, u32[]{:S(2)}, u32[]{:S(2)}) collective-permute-start(f32[2,256]{1,0:T(2,128)S(1)} %get-tuple-element.22.refs_3_), channel_id=1, source_target_pairs={{0,8},{4,12},{8,0},{12,4},{1,9},{5,13},{9,1},{13,5},{2,10},{6,14},... | collective-permute-start | bytes 6152 | tf_op jit(solution)/shard_map/ppermute | solution.py:475
  8.3 2.4 %collective-permute-start.2 = (f32[2,256]{1,0:T(2,128)S(1)}, f32[2,256]{1,0:T(2,128)S(1)}, u32[]{:S(2)}, u32[]{:S(2)}) collective-permute-start(f32[2,256]{1,0:T(2,128)S(1)} %get-tuple-element.22.refs_3_), channel_id=1, source_target_pairs={{0,4},{4,0},{8,12},{12,8},{1,5},{5,1},{9,13},{13,9},{2,6},{6,2},{1... | collective-permute-start | bytes 6152 | tf_op jit(solution)/shard_map/ppermute | solution.py:475
  32.7 2.2 %collective-permute-start.5 = (f32[16,8,128]{2,1,0:T(8,128)S(1)}, f32[16,8,128]{2,1,0:T(8,128)S(1)}, u32[]{:S(2)}, u32[]{:S(2)}) collective-permute-start(f32[16,8,128]{2,1,0:T(8,128)S(1)} %get-tuple-element.30), channel_id=1, source_target_pairs={{0,4},{4,0},{8,12},{12,8},{1,5},{5,1},{9,13},{13,9},{2,6},{6,2},{1... | collective-permute-start | bytes 196616 | tf_op jit(solution)/shard_map/ppermute | solution.py:531
  33.0 3.5 %collective-permute-start.6 = (f32[16,8,128]{2,1,0:T(8,128)S(1)}, f32[16,8,128]{2,1,0:T(8,128)S(1)}, u32[]{:S(2)}, u32[]{:S(2)}) collective-permute-start(f32[16,8,128]{2,1,0:T(8,128)S(1)} %get-tuple-element.31), channel_id=1, source_target_pairs={{0,8},{4,12},{8,0},{12,4},{1,9},{5,13},{9,1},{13,5},{2,10},{6,14},... | collective-permute-start | bytes 196616 | tf_op jit(solution)/shard_map/ppermute | solution.py:531
  34.3 4.0 %collective-permute-start.7 = (f32[16,8,128]{2,1,0:T(8,128)S(1)}, f32[16,8,128]{2,1,0:T(8,128)S(1)}, u32[]{:S(2)}, u32[]{:S(2)}) collective-permute-start(f32[16,8,128]{2,1,0:T(8,128)S(1)} %get-tuple-element.32), channel_id=1, source_target_pairs={{0,12},{4,8},{8,4},{12,0},{1,13},{5,9},{9,5},{13,1},{2,14},{6,10},... | collective-permute-start | bytes 196616 | tf_op jit(solution)/shard_map/ppermute | solution.py:531

commit v5 on v4

--- a/solution.py
+++ b/solution.py
@@ -10,6 +10,7 @@
 HALO = 2 * REACH
 PACK = 8
 PIECE = 2
+FEW = 4
 NET = PACK - 2
 OFF = -1e30
 VMEM_LIMIT = 44 * 2**20
@@ -157,7 +158,7 @@
     outs = refs[9 + tm : 9 + 2 * tm]
     (
         rows_s, par_s, held_s, start_s, common_s, points_s, hid2_s, inputs_s, chunk_s,
-        in_bias, mid_bias, eps_s, parts_s, turned_s, low_s,
+        in_bias, mid_bias, eps_s, parts_s, turned_s, low_s, last_s,
     ) = refs[9 + 2 * tm :]
     rows, chans, depth = mid_ref.shape
     states, hid = par_s.shape[0], par_s.shape[1] // 2
@@ -252,41 +253,40 @@
                 hid2_s[i, place, :hid] = high
                 hid2_s[i, place, hid:] = low
 
-    def noise(packs, width):
-        units = PACK // 2 + (NET // 2) * (packs - 1)
+    def unit_taps(first, count):
+        units = range(first, first + count)
         left = jnp.concatenate(
-            [
-                jnp.concatenate([hid2_s[2 * u + k] for u in range(units)], 0)
-                for k in range(4)
-            ],
-            1,
+            [jnp.concatenate([hid2_s[2 * u + k] for u in units], 0) for k in range(4)], 1
         )
         taps = jnp.dot(left, wo_ref[...], preferred_element_type=F32)
-        taps = (taps[:, :hid] + taps[:, hid:]).reshape(units, wide, states, hid)
-        shape = (width, states, hid)
-        group = lane_groups(shape, 2 * chans)
-        one = [
-            jnp.where(
-                group == 1,
-                taps[u, 1 : width + 1],
-                jnp.where(group == 2, taps[u, 2 : width + 2], taps[u, :width]),
-            )
-            for u in range(units)
-        ]
-
-        def turn(value, shift):
-            return pltpu.roll(value.reshape(width * states, hid), shift, 1).reshape(shape)
-
-        lower, even = group < 2, group % 2 == 0
-        values = []
-        for p in range(packs):
-            u0, u1, u2, u3 = one[NET // 2 * p : NET // 2 * p + 4]
+        taps = taps.reshape(count, wide, states, 2 * hid)
+        return [taps[u] for u in range(count)]
+
+    def noise(taps, width, use):
+        def work(first, last):
+            size = last - first
+            shape = (size, states, hid)
+            group = lane_groups(shape, 2 * chans)
+            one = []
+            for unit in taps:
+                both = unit[first : last + 2]
+                both = both[:, :, :hid] + both[:, :, hid:]
+                rest = jnp.where(group == 2, both[2:], both[:size])
+                one.append(jnp.where(group == 1, both[1 : size + 1], rest))
+
+            def turn(value, shift):
+                return pltpu.roll(value.reshape(size * states, hid), shift, 1).reshape(shape)
+
+            lower, even = group < 2, group % 2 == 0
+            u0, u1, u2, u3 = one
             v0 = jnp.where(lower, u0, u2) + turn(jnp.where(lower, u2, u0), hid // 2)
             v1 = jnp.where(lower, u1, u3) + turn(jnp.where(lower, u3, u1), hid // 2)
             other = jnp.where(even, v1, v0)
             other = jnp.where(even, turn(other, hid - 2 * chans), turn(other, 2 * chans))
-            values.append(jnp.where(even, v0, v1) + other + out_bias)
-        return values
+            use(first, last, jnp.where(even, v0, v1) + other + out_bias)
+
+        for first in range(0, width, FEW):
+            work(first, min(first + FEW, width))
 
     state = lax.broadcasted_iota(jnp.int32, (1, states, hid), 1)
 
@@ -329,75 +329,95 @@
 
         to_points(i, field, field(groups, groups + 1))
 
+    packs = inputs_s.shape[0]
+    for p in range(packs):
+        start_s[p] = packed_start(REACH + NET * p)
+        inputs_s[p, reach_cols * states :] = jnp.zeros(((wide - reach_cols) * states, hid), F32)
+    group = lane_groups((1, hid), chans)
+
+    def next_inputs(p, first, last, value):
+        start = start_s[p, REACH + first : REACH + last]
+        start = jnp.broadcast_to(start[:, None, :], (last - first, states, hid))
+        row = group + (row0 - REACH + NET * p)
+        keep = jnp.where((row >= 0) & (row < all_rows), 1.0, 0.0)
+        drift = drift_x[None] * start + eps_s[first:last] * (value * keep)
+        total = start + earlier(drift)
+        inputs_s[p, first * states : last * states] = total.reshape((last - first) * states, hid)
+
+    none = jnp.zeros((1, 4, states, hid), F32)
+
+    def next_points(p):
+        behind = none
+        for first, last in reversed(pieces(groups)):
+            size = (last - first) * states
+            fours = inputs_s[p, 4 * first * states : 4 * last * states]
+            fours = fours.reshape(last - first, 4, states, hid)
+            place = slice((p * groups + first) * states, (p * groups + last) * states)
+            for point, form in enumerate(column_points(fours, behind)):
+                value = form.reshape(size, hid)
+                parts_s[point, place] = value
+                turned_s[point, place] = pltpu.roll(value, hid // 2, 1)
+                low_s[point, place] = split(value)[1]
+            behind = fours
+
+    def second_rows(p, pair):
+        own = slice(p * groups * states, (p + 1) * groups * states)
+        products = []
+        for point in range(6):
+            left = left_side(pair, parts_s[point, own], turned_s[point, own], low_s[point, own])
+            both = jnp.dot(left, wi_forms[pair, point], preferred_element_type=F32)
+            products.append(both.reshape(groups, states, 2 * hid))
+        for r in range(2):
+            i = NET * p + 2 * pair + r
+            ok = in_field(row0 - 2 + i)
+
+            def field(first, last, r=r, ok=ok):
+                parts = [m[first:last, :, r * hid : (r + 1) * hid] for m in products]
+                value = jnp.stack(column_outputs(*parts), 1)
+                bias = in_bias[ok, 3 + 4 * first : 3 + 4 * last].reshape(value.shape)
+                return silu_of_double(value + bias)
+
+            to_points(i, field, none)
+
+    def last_drifts(first, last, value):
+        size = (last - first) * states
+        place = slice((REACH + first) * states, (REACH + last) * states)
+        inputs = jnp.where(
+            lane_groups((size, hid), chans) < PACK - REACH,
+            pltpu.roll(inputs_s[0, place], hid - REACH * chans, 1),
+            pltpu.roll(inputs_s[1, place], (NET - REACH) * chans, 1),
+        ).reshape(value.shape)
+        drift = drift_x[None] * inputs + drift_eps[None] * value
+        last_s[first * states : last * states] = drift.reshape(size, hid)
+
     step = 4
     calls = [functools.partial(first_points, i) for i in range(rows + 10)]
     for call in calls[: step + 2]:
         call()
+    taps, packs_ready = [], 0
+
+    def second_inputs():
+        p = packs_ready
+        first = NET // 2 * p
+        noise(taps[first : first + 4], reach_cols, functools.partial(next_inputs, p))
+        next_points(p)
+        for pair in range(NET // 2):
+            second_rows(p, pair)
+
     for first in range(0, rows + 8, step):
         ahead = first + step + 2
         second_hidden(range(first, first + step), -4, 0, calls[ahead : ahead + step])
-
-    packs = inputs_s.shape[0]
-    value = noise(packs, reach_cols)
-    group = lane_groups((1, hid), chans)
-    for p in range(packs):
-        start = packed_start(REACH + NET * p)[REACH : REACH + reach_cols]
-        start = jnp.broadcast_to(start[:, None, :], (reach_cols, states, hid))
-        row = group + (row0 - REACH + NET * p)
-        keep = jnp.where((row >= 0) & (row < all_rows), 1.0, 0.0)
-        drift = drift_x[None] * start + eps_s[...] * (value[p] * keep)
-        total = (start + earlier(drift)).reshape(reach_cols * states, hid)
-        inputs_s[p, : reach_cols * states] = total
-        inputs_s[p, reach_cols * states :] = jnp.zeros(((wide - reach_cols) * states, hid), F32)
-
-    fours = wide // 4 - 1
-    packed = [inputs_s[p].reshape(groups, 4, states, hid) for p in range(packs)]
-    packed = [column_points(v[:fours], v[fours:]) for v in packed]
-    for point, form in enumerate(zip(*packed)):
-        value = jnp.stack(form).reshape(packs * fours * states, hid)
-        parts_s[point] = value
-        turned_s[point] = pltpu.roll(value, hid // 2, 1)
-        low_s[point] = split(value)[1]
-
-    def second_rows(pair):
-        products = []
-        for point in range(6):
-            left = left_side(pair, parts_s[point], turned_s[point], low_s[point])
-            both = jnp.dot(left, wi_forms[pair, point], preferred_element_type=F32)
-            products.append(both.reshape(packs, fours, states, 2 * hid))
-        for p in range(packs):
-            for r in range(2):
-                i = NET * p + 2 * pair + r
-                ok = in_field(row0 - 2 + i)
-
-                def field(first, last, p=p, r=r, ok=ok):
-                    last = min(last, fours)
-                    parts = [m[p, first:last, :, r * hid : (r + 1) * hid] for m in products]
-                    value = jnp.stack(column_outputs(*parts), 1)
-                    bias = in_bias[ok, 3 + 4 * first : 3 + 4 * last].reshape(value.shape)
-                    value = silu_of_double(value + bias)
-                    return jnp.concatenate([value, none], 0) if last == fours else value
-
-                none = jnp.zeros((1, 4, states, hid), F32)
-                to_points(i, field, none)
-
-    calls = [functools.partial(second_rows, pair) for pair in range(NET // 2)]
-    calls[0]()
-    calls[1]()
-    second_hidden([0, 1, NET, NET + 1], -1, 3, calls[2:])
-    second_hidden([2, 3, 4, 5, NET + 2, NET + 3], -1, 3)
-
-    value = noise(1, cols)[0]
-    size = cols * states
-    upper = inputs_s[0, REACH * states : REACH * states + size]
-    lower = inputs_s[1, REACH * states : REACH * states + size]
-    inputs = jnp.where(
-        lane_groups((size, hid), chans) < PACK - REACH,
-        pltpu.roll(upper, hid - REACH * chans, 1),
-        pltpu.roll(lower, (NET - REACH) * chans, 1),
-    ).reshape(cols, states, hid)
-    drift = drift_x[None] * inputs + drift_eps[None] * value
-    high, low = split(drift.reshape(size, hid).T)
+        if len(taps) >= NET // 2 * packs_ready + 4:
+            second_inputs()
+            packs_ready += 1
+        taps += unit_taps(len(taps), (first + step - 2) // 2 - len(taps))
+    second_hidden(range(step), -1, 3)
+    second_inputs()
+    taps = unit_taps(0, 1)
+    second_hidden(range(step, rows + 2), -1, 3)
+    taps += unit_taps(1, 3)
+    noise(taps, cols, last_drifts)
+    high, low = split(last_s[...].T)
     total = jnp.dot(high, sums_ref[...], preferred_element_type=F32) + jnp.dot(
         low, sums_ref[...], preferred_element_type=F32
     )
@@ -503,7 +523,7 @@
     groups = (cols + 8) // 4
     wide = 4 * groups
     width = here * cols
-    parts = (rows + HALO - 2) // NET * (groups - 1) * states
+    parts = (rows + HALO - 2) // NET * groups * states
     chunks = kernel_call(
         functools.partial(main_kernel, tm),
         tuple(local((chans, rows, width), F32) for _ in range(tm)),
@@ -522,6 +542,7 @@
             pltpu.VMEM((2, wide + 3, states, hid), F32),
             pltpu.VMEM((cols + HALO, states, hid), F32),
             *(pltpu.VMEM((6, parts, hid), kind) for kind in (F32, F32, BF16)),
+            pltpu.VMEM((cols * states, hid), F32),
         ),
         flops=10**10,
         read=8 * 10**6,

time: 39.3 us -> 35.4 us (0.901)
  Pallas kernels: 26 us -> 22.1 us
    pallas_call x1, Pallas kernels: 22 us -> 18 us  [on_device(): kernel_call(functools.partial(main_kernel, tm), tuple((local((chans, rows...]
  transfers between devices with their start and end apart: 8 -> 8, of which waited for: 2 -> 2; matrix products, arithmetic and copies ran while one was open for 0% -> 0% of each run, Pallas kernels for 5% -> 6%
where the time goes in v5:
time: 35.4 us; the launch traced here: 35.2 us
  Pallas kernels  22.1 us (62%)
  starting transfers between devices  9.62 us (27%)
  waiting for transfers between devices  3.44 us (10%)
    pallas_call x1, Pallas kernels, on_device(): kernel_call(functools.partial(main_kernel, tm), tuple((local((chans, rows...  18 us
    ppermute x1, starting transfers between devices, on_device(): odd = lax.ppermute(odd, 'space', pairs + [(b, a) for a, b in pairs])  4.48 us
    ppermute x3, waiting for transfers between devices, on_device(): lax.ppermute(chunks[k], 'tm', [(i, i ^ k) for i in range(tm)])  3.42 us
    ppermute x3, starting transfers between devices, on_device(): lax.ppermute(par, 'tm', [(i, i ^ k) for i in range(tm)])  2.87 us
    ppermute x3, starting transfers between devices, on_device(): lax.ppermute(chunks[k], 'tm', [(i, i ^ k) for i in range(tm)])  2.21 us
    pallas_call x1, Pallas kernels, on_device(): kernel_call(functools.partial(weights_kernel, states), (local((NET // 2,...  2.1 us
    pallas_call x1, Pallas kernels, on_device(): kernel_call(pack_kernel, (local((rows, chans, depth), F32), edge, edge, l...  1.12 us
    pallas_call x1, Pallas kernels, on_device(): kernel_call(functools.partial(join_kernel, tm), shape((here, chans, rows,...  0.86 us
  transfers between devices with their start and end apart: 8, of which 2 were waited for; matrix products, arithmetic and copies ran while one was open for 0% of the time, Pallas kernels for 6%

profile of v5, /device:TPU:9, one launch (start us, length us, event | category | flops | bytes accessed | tf_op | source)
XLA Modules:
  0.0 35.2 jit_solution(384415476266947777)
XLA Ops:
  0.0 1.1 %shard_map.100 = (f32[8,16,128]{2,1,0:T(8,128)S(1)}, f32[6,16,128]{2,1,0:T(8,128)S(1)}, f32[6,16,128]{2,1,0:T(8,128)S(1)}, f32[2,256]{1,0:T(2,128)S(1)}) custom-call(f32[16,8,256]{2,1,0:T(8,128)} %refs_0_.1, f32[2,128]{1,0:T(2,128)} %refs_1_.2, f32[2]{0:T(128)} %refs_2_.2, f32[2]{0:T(128)} %refs_3_.2), custom_call_target="tpu_custom_call" | custom-call | bytes 1000000 | tf_op jit(solution)/shard_map/pallas_call | solution.py:478
  1.1 0.1 collective-permute-start
  1.2 4.5 %collective-permute-start.1 = (f32[6,16,128]{2,1,0:T(8,128)S(1)}, f32[6,16,128]{2,1,0:T(8,128)S(1)}, u32[]{:S(2)}, u32[]{:S(2)}) collective-permute-start(f32[6,16,128]{2,1,0:T(8,128)S(1)} %get-tuple-element.21), channel_id=1, source_target_pairs={{1,2},{2,1},{5,6},{6,5},{9,10},{10,9},{13,14},{14,13},{17,18},{18,... | collective-permute-start | bytes 147464 | tf_op jit(solution)/shard_map/ppermute | solution.py:493
  5.7 2.4 %collective-permute-start.4 = (f32[2,256]{1,0:T(2,128)S(1)}, f32[2,256]{1,0:T(2,128)S(1)}, u32[]{:S(2)}, u32[]{:S(2)}) collective-permute-start(f32[2,256]{1,0:T(2,128)S(1)} %get-tuple-element.22.refs_3_), channel_id=1, source_target_pairs={{0,12},{4,8},{8,4},{12,0},{1,13},{5,9},{9,5},{13,1},{2,14},{6,10},... | collective-permute-start | bytes 6152 | tf_op jit(solution)/shard_map/ppermute | solution.py:495
  8.1 0.3 collective-permute-start.3
  8.3 0.2 collective-permute-start.2
  8.6 2.1 %shard_map.101 = (bf16[3,256,768]{2,1,0:T(8,128)(2,1)S(1)}, bf16[3,6,256,256]{3,2,1,0:T(8,128)(2,1)S(1)}, bf16[6,768,256]{2,1,0:T(8,128)(2,1)S(1)}, bf16[1024,25...) custom-call(f32[3,3,16,128]{3,2,1,0:T(8,128)} %bitcast.1, f32[3,3,128,128]{3,2,1,0:T(8,128)} %refs_1_.3, ...), custom_call_target="tpu_custom_call" | custom-call | flops 10000000 | bytes 8000000 | tf_op jit(solution)/shard_map/pallas_call | solution.py:498
  10.7 0.0 collective-permute-done.4.refs_6_
  10.7 0.0 collective-permute-done.3.refs_5_
  10.7 0.0 collective-permute-done.2.refs_4_
  10.7 0.0 collective-permute-done.refs_1_
  10.7 0.0 collective-permute-done.1.refs_2_
  10.7 18.0 %shard_map.102 = (f32[16,8,128]{2,1,0:T(8,128)S(1)}, f32[16,8,128]{2,1,0:T(8,128)S(1)}, f32[16,8,128]{2,1,0:T(8,128)S(1)}, f32[16,8,128]{2,1,0:T(8,128)S(1)}) custom-call(f32[8,16,128]{2,1,0:T(8,128)S(1)} %get-tuple-element.19.refs_0_, f32[6,16,128]{2,1,0:T(8,128)S(1)} %collective-permute-done.refs_1_, f32[6,16,128]{2,1,0:T(8,128)S(1)} %collective-permute-done.1.refs_2_, ...), custom_call_target="tpu_custom_call" | custom-call | flops 10000000000 | bytes 8000000 | tf_op jit(solution)/shard_map/pallas_call | solution.py:527
  28.7 0.4 %collective-permute-start.5 = (f32[16,8,128]{2,1,0:T(8,128)S(1)}, f32[16,8,128]{2,1,0:T(8,128)S(1)}, u32[]{:S(2)}, u32[]{:S(2)}) collective-permute-start(f32[16,8,128]{2,1,0:T(8,128)S(1)} %get-tuple-element.30), channel_id=1, source_target_pairs={{0,4},{4,0},{8,12},{12,8},{1,5},{5,1},{9,13},{13,9},{2,6},{6,2},{1... | collective-permute-start | bytes 196616 | tf_op jit(solution)/shard_map/ppermute | solution.py:552
  29.1 1.2 %collective-permute-start.6 = (f32[16,8,128]{2,1,0:T(8,128)S(1)}, f32[16,8,128]{2,1,0:T(8,128)S(1)}, u32[]{:S(2)}, u32[]{:S(2)}) collective-permute-start(f32[16,8,128]{2,1,0:T(8,128)S(1)} %get-tuple-element.31), channel_id=1, source_target_pairs={{0,8},{4,12},{8,0},{12,4},{1,9},{5,13},{9,1},{13,5},{2,10},{6,14},... | collective-permute-start | bytes 196616 | tf_op jit(solution)/shard_map/ppermute | solution.py:552
  30.3 0.6 %collective-permute-start.7 = (f32[16,8,128]{2,1,0:T(8,128)S(1)}, f32[16,8,128]{2,1,0:T(8,128)S(1)}, u32[]{:S(2)}, u32[]{:S(2)}) collective-permute-start(f32[16,8,128]{2,1,0:T(8,128)S(1)} %get-tuple-element.32), channel_id=1, source_target_pairs={{0,12},{4,8},{8,4},{12,0},{1,13},{5,9},{9,5},{13,1},{2,14},{6,10},... | collective-permute-start | bytes 196616 | tf_op jit(solution)/shard_map/ppermute | solution.py:552
  30.9 0.0 collective-permute-done.5.refs_1_
  30.9 1.6 %collective-permute-done.6.refs_2_ = f32[16,8,128]{2,1,0:T(8,128)S(1)} collective-permute-done((f32[16,8,128]{2,1,0:T(8,128)S(1)}, f32[16,8,128]{2,1,0:T(8,128)S(1)}, u32[]{:S(2)}, u32[]{:S(2)}) %collective-permute-start.6) | collective-permute-done | bytes 65568 | tf_op jit(solution)/shard_map/ppermute | solution.py:552
  32.6 1.8 %collective-permute-done.7.refs_3_ = f32[16,8,128]{2,1,0:T(8,128)S(1)} collective-permute-done((f32[16,8,128]{2,1,0:T(8,128)S(1)}, f32[16,8,128]{2,1,0:T(8,128)S(1)}, u32[]{:S(2)}, u32[]{:S(2)}) %collective-permute-start.7) | collective-permute-done | bytes 65568 | tf_op jit(solution)/shard_map/ppermute | solution.py:552
  34.4 0.9 %shard_map.103 = f32[2,16,8,256]{3,2,1,0:T(8,128)} custom-call(f32[16,8,128]{2,1,0:T(8,128)S(1)} %get-tuple-element.29.refs_0_, f32[16,8,128]{2,1,0:T(8,128)S(1)} %collective-permute-done.5.refs_1_, f32[16,8,128]{2,1,0:T(8,128)S(1)} %collective-permute-done.6.refs_2_, f32[16,8,128]{2,1,0:T(8,128)S(1)} %collective-permute-done.7.refs_3_), custom_call_target="tpu_custom_call" | custom-call | bytes 1000000 | tf_op jit(solution)/shard_map/pallas_call | solution.py:554
Async XLA Ops:
  1.1 9.6 %collective-permute-start = (f32[6,16,128]{2,1,0:T(8,128)S(1)}, f32[6,16,128]{2,1,0:T(8,128)S(1)}, u32[]{:S(2)}, u32[]{:S(2)}) collective-permute-start(f32[6,16,128]{2,1,0:T(8,128)S(1)} %get-tuple-element.20), channel_id=1, source_target_pairs={{0,1},{1,0},{2,3},{3,2},{4,5},{5,4},{6,7},{7,6},{8,9},{9,8},{10,11... | collective-permute-start | bytes 147464 | tf_op jit(solution)/shard_map/ppermute | solution.py:491
  1.2 9.5 %collective-permute-start.1 = (f32[6,16,128]{2,1,0:T(8,128)S(1)}, f32[6,16,128]{2,1,0:T(8,128)S(1)}, u32[]{:S(2)}, u32[]{:S(2)}) collective-permute-start(f32[6,16,128]{2,1,0:T(8,128)S(1)} %get-tuple-element.21), channel_id=1, source_target_pairs={{1,2},{2,1},{5,6},{6,5},{9,10},{10,9},{13,14},{14,13},{17,18},{18,... | collective-permute-start | bytes 147464 | tf_op jit(solution)/shard_map/ppermute | solution.py:493
  5.7 5.0 %collective-permute-start.4 = (f32[2,256]{1,0:T(2,128)S(1)}, f32[2,256]{1,0:T(2,128)S(1)}, u32[]{:S(2)}, u32[]{:S(2)}) collective-permute-start(f32[2,256]{1,0:T(2,128)S(1)} %get-tuple-element.22.refs_3_), channel_id=1, source_target_pairs={{0,12},{4,8},{8,4},{12,0},{1,13},{5,9},{9,5},{13,1},{2,14},{6,10},... | collective-permute-start | bytes 6152 | tf_op jit(solution)/shard_map/ppermute | solution.py:495
  8.1 2.6 %collective-permute-start.3 = (f32[2,256]{1,0:T(2,128)S(1)}, f32[2,256]{1,0:T(2,128)S(1)}, u32[]{:S(2)}, u32[]{:S(2)}) collective-permute-start(f32[2,256]{1,0:T(2,128)S(1)} %get-tuple-element.22.refs_3_), channel_id=1, source_target_pairs={{0,8},{4,12},{8,0},{12,4},{1,9},{5,13},{9,1},{13,5},{2,10},{6,14},... | collective-permute-start | bytes 6152 | tf_op jit(solution)/shard_map/ppermute | solution.py:495
  8.3 2.4 %collective-permute-start.2 = (f32[2,256]{1,0:T(2,128)S(1)}, f32[2,256]{1,0:T(2,128)S(1)}, u32[]{:S(2)}, u32[]{:S(2)}) collective-permute-start(f32[2,256]{1,0:T(2,128)S(1)} %get-tuple-element.22.refs_3_), channel_id=1, source_target_pairs={{0,4},{4,0},{8,12},{12,8},{1,5},{5,1},{9,13},{13,9},{2,6},{6,2},{1... | collective-permute-start | bytes 6152 | tf_op jit(solution)/shard_map/ppermute | solution.py:495
  28.7 2.2 %collective-permute-start.5 = (f32[16,8,128]{2,1,0:T(8,128)S(1)}, f32[16,8,128]{2,1,0:T(8,128)S(1)}, u32[]{:S(2)}, u32[]{:S(2)}) collective-permute-start(f32[16,8,128]{2,1,0:T(8,128)S(1)} %get-tuple-element.30), channel_id=1, source_target_pairs={{0,4},{4,0},{8,12},{12,8},{1,5},{5,1},{9,13},{13,9},{2,6},{6,2},{1... | collective-permute-start | bytes 196616 | tf_op jit(solution)/shard_map/ppermute | solution.py:552
  29.1 3.5 %collective-permute-start.6 = (f32[16,8,128]{2,1,0:T(8,128)S(1)}, f32[16,8,128]{2,1,0:T(8,128)S(1)}, u32[]{:S(2)}, u32[]{:S(2)}) collective-permute-start(f32[16,8,128]{2,1,0:T(8,128)S(1)} %get-tuple-element.31), channel_id=1, source_target_pairs={{0,8},{4,12},{8,0},{12,4},{1,9},{5,13},{9,1},{13,5},{2,10},{6,14},... | collective-permute-start | bytes 196616 | tf_op jit(solution)/shard_map/ppermute | solution.py:552
  30.3 4.0 %collective-permute-start.7 = (f32[16,8,128]{2,1,0:T(8,128)S(1)}, f32[16,8,128]{2,1,0:T(8,128)S(1)}, u32[]{:S(2)}, u32[]{:S(2)}) collective-permute-start(f32[16,8,128]{2,1,0:T(8,128)S(1)} %get-tuple-element.32), channel_id=1, source_target_pairs={{0,12},{4,8},{8,4},{12,0},{1,13},{5,9},{9,5},{13,1},{2,14},{6,10},... | collective-permute-start | bytes 196616 | tf_op jit(solution)/shard_map/ppermute | solution.py:552
